TPU v7x, 512 devices: a whole 4x4x16 slice. The times are simulated.
512 devices in a mesh: frame: 32 (over y, z_lo, core), patch: 16 (over x, z_hi).
Axes of the slice: x: 4, y: 4, z: 16 (z_hi: 4, z_lo: 4; z = z_hi * 4 + z_lo), core: 2. Of those that a mesh axis runs over, the one named last changes fastest.
Arguments:
- tokens: bfloat16 [32, 2048, 1152], P('frame', 'patch'), may hold values from -700 to 700, as said below
- key_frame: int32 [1], replicated, may hold values from 0 to 31
- qkv_spatial: bfloat16 [1152, 3456], P(None, 'patch'), may hold values from -10 to 10
- out_spatial: bfloat16 [1152, 1152], replicated, may hold values from -0.75 to 0.75
- qkv_temporal: bfloat16 [1152, 3456], P(None, 'patch'), may hold values from -10 to 10
Outputs:
- spatial_out: bfloat16 [32, 2048, 1152], P('frame', 'patch')
- temporal_out: bfloat16 [32, 2048, 1152], P('frame', 'patch')
Inputs may be any that keep to these rules, and one draw needn't show every extreme that they name: `tokens`: patch features.
All inputs are finite; a program needn't handle non-finite values.
Results may differ from a plain program's by a relative error of at most 0.024.
Values may be sent and summed in bfloat16 or wider, within the bound.
A program may use at most 64 MiB of HBM per device.

v0:
```python
from functools import partial

import jax
import jax.numpy as jnp
from jax import lax
from jax.sharding import PartitionSpec as P

HEAD_DIM = 72


epsilon = 1e-06


def broadcast(x, axis, root):
    mine = lax.axis_index(axis) == root
    return lax.psum(jnp.where(mine, x, jnp.zeros_like(x)), axis)


def rms_norm(values):
    values = values.astype(jnp.float32)
    return values * lax.rsqrt(jnp.mean(values * values, axis=-1, keepdims=True) + epsilon)


def softmax_weights(scores):
    largest = jnp.max(scores, axis=-1, keepdims=True)
    exponent = jnp.exp(scores - largest)
    return (exponent / jnp.sum(exponent, axis=-1, keepdims=True)).astype(jnp.bfloat16)


def key_scores(query_block, key_rows, score_scale):
    return (
        lax.dot_general(
            query_block, key_rows, (((1,), (1,)), ((), ())), preferred_element_type=jnp.float32
        )
        * score_scale
    )


def joint_block(query_block, all_keys, all_values, score_scale):
    weights = softmax_weights(key_scores(query_block, all_keys, score_scale))
    return jnp.dot(weights, all_values, preferred_element_type=jnp.float32).astype(jnp.bfloat16)


def temporal_attend(block_qkv, local_heads, score_scale):
    frames = block_qkv.shape[0]
    patch_count = block_qkv.shape[2]
    split_qkv = block_qkv[:, 0].reshape(frames, patch_count, local_heads, 3, HEAD_DIM)
    scores = (
        jnp.einsum(
            "fnhc,gnhc->nhfg",
            split_qkv[:, :, :, 0],
            split_qkv[:, :, :, 1],
            preferred_element_type=jnp.float32,
        )
        * score_scale
    )
    weights = softmax_weights(scores)
    attended = jnp.einsum(
        "nhfg,gnhc->fnhc", weights, split_qkv[:, :, :, 2], preferred_element_type=jnp.float32
    )
    return attended.astype(jnp.bfloat16).reshape(frames, 1, patch_count, local_heads * HEAD_DIM)


def per_device(tokens, key_frame, qkv_spatial, out_spatial, qkv_temporal):
    score_scale = HEAD_DIM ** (-0.5)
    local_heads = qkv_temporal.shape[1] // (3 * HEAD_DIM)
    normed = rms_norm(tokens[0]).astype(jnp.bfloat16)
    spatial_qkv = jnp.dot(
        lax.all_gather(normed, "patch", axis=0, tiled=True),
        qkv_spatial,
        preferred_element_type=jnp.float32,
    ).astype(jnp.bfloat16)
    patch_count = spatial_qkv.shape[0]
    grouped = spatial_qkv.reshape(patch_count, local_heads, 3, HEAD_DIM)
    own_pairs = grouped[:, :, 1:].reshape(patch_count, local_heads * 2 * HEAD_DIM)
    key_pairs = broadcast(own_pairs, "frame", key_frame[0])
    key_pairs = key_pairs.reshape(patch_count, local_heads, 2, HEAD_DIM)
    block_rows = min(512, patch_count)
    block_count = patch_count // block_rows
    query_blocks = grouped[:, 0, 0].reshape(block_count, block_rows, HEAD_DIM)
    own_keys = grouped[:, 0, 1]
    own_values = grouped[:, 0, 2]
    frame_keys = key_pairs[:, 0, 0]
    frame_values = key_pairs[:, 0, 1]
    all_keys = jnp.concatenate([own_keys, frame_keys], axis=0)
    all_values = jnp.concatenate([own_values, frame_values], axis=0)
    attended = lax.map(
        partial(joint_block, all_keys=all_keys, all_values=all_values, score_scale=score_scale),
        query_blocks,
    )
    outputs = attended.reshape(patch_count, HEAD_DIM)
    token_heads = lax.all_to_all(outputs, "patch", split_axis=0, concat_axis=1, tiled=True)
    spatial = jnp.dot(token_heads, out_spatial, preferred_element_type=jnp.float32).astype(
        jnp.bfloat16
    )
    temporal_in = rms_norm(spatial).astype(jnp.bfloat16)
    temporal_qkv = jnp.dot(
        lax.all_gather(temporal_in, "patch", axis=0, tiled=True),
        qkv_temporal,
        preferred_element_type=jnp.float32,
    ).astype(jnp.bfloat16)
    frame_count = lax.axis_size("frame")
    group_rows = patch_count // frame_count
    grouped_qkv = temporal_qkv.reshape(1, frame_count, group_rows, temporal_qkv.shape[1])
    mixed_heads = temporal_attend(
        lax.all_to_all(grouped_qkv, "frame", split_axis=1, concat_axis=0, tiled=True),
        local_heads=local_heads,
        score_scale=score_scale,
    )
    mixed_heads = mixed_heads.reshape(frame_count, group_rows, local_heads * HEAD_DIM)
    temporal = lax.all_to_all(
        lax.all_to_all(mixed_heads, "frame", split_axis=0, concat_axis=1, tiled=True),
        "patch",
        split_axis=1,
        concat_axis=2,
        tiled=True,
    )
    return (spatial[None], temporal)


def solution(mesh):
    return jax.shard_map(
        per_device,
        mesh=mesh,
        in_specs=(P("frame", "patch", None), P(), P(None, "patch"), P(), P(None, "patch")),
        out_specs=(P("frame", "patch", None), P("frame", "patch", None)),
        check_vma=False,
    )
```

profile of v0, /device:TPU:1, one launch (start us, length us, event | category | flops | bytes accessed | tf_op | source)
XLA Modules:
  0.0 798.2 jit_solution(4848338679873683103)
XLA Ops:
  7.2 0.0 copy-start
  7.2 0.0 all-gather.3.cloned.1.call-start
  7.2 1.3 fusion.16
  8.5 1.8 fusion.17
  10.3 0.0 all-gather.3.cloned.1.call-update
  10.3 0.0 all-reduce.2.cloned.1.call-start
  11.0 149.2 %all-gather.3.cloned.1.call-done = bf16[2048,1152]{1,0:T(8,128)(2,1)} async-done(((bf16[128,1152]{1,0:T(8,128)(2,1)}), bf16[2048,1152]{1,0:T(8,128)(2,1)}) %all-gather.3.cloned.1.call-update) | async-done | bytes 4718608 | tf_op jit(solution)/shard_map/all_gather | solution.py:69
  160.2 4.2 convolution_convert_fusion.1
  164.4 0.8 slice.38
  165.2 2.2 copy.48
  167.4 2.3 broadcast_select_fusion
  169.8 0.0 all-reduce.2.cloned.1.call-update
  169.8 0.0 all-gather.5.cloned.1.call-start
  169.8 0.9 fusion.22
  170.8 2.0 copy.47
  172.8 2.0 copy.49
  174.8 1.2 copy.26
  176.0 279.0 %all-reduce.2.cloned.1.call-done = bf16[2048,1,2,72]{3,0,2,1:T(8,128)(2,1)} async-done(((bf16[2048,1,2,72]{3,0,2,1:T(8,128)(2,1)}), bf16[2048,1,2,72]{3,0,2,1:T(8,128)(2,1)}) %all-reduce.2.cloned.1.call-update) | async-done | bytes 589840 | tf_op jit(solution)/shard_map/psum | solution.py:16
  455.0 1.3 slice_bitcast_fusion
  456.3 3.0 pad_maximum_fusion
  459.2 26.0 %while.10 = (s32[]{:T(128)}, bf16[4,512,72]{1,2,0:T(8,128)(2,1)S(1)}, bf16[4,512,72]{2,1,0:T(8,128)(2,1)S(1)}, bf16[4096,72]{1,0:T(8,128)(2,1)}, bf16[4096,72]{1,0:T(8,128)(2,1)}, /*index=5*/s32[]{:T(128)}) while((s32[]{:T(128)}, bf16[4,512,72]{1,2,0:T(8,128)(2,1)S(1)}, bf16[4,512,72]{2,1,0:T(8,128)(2,1)S(1)}, bf16[4096,72]{1,0:T(8,128)(2,1)}, ...), condition=%wide.region_5.6_spmd, body=%wide.region_2.5_spmd.sunk | while | flops 622889984 | bytes 29378664 | solution.py:87
  459.2 2.6 multiply_reduce_fusion.2
  461.8 1.5 fusion.39
  463.3 2.4 fusion.40
  465.7 2.6 multiply_reduce_fusion.2
  468.3 1.5 fusion.39
  469.8 2.4 fusion.40
  472.2 2.6 multiply_reduce_fusion.2
  474.8 1.5 fusion.39
  476.3 2.4 fusion.40
  478.7 2.6 multiply_reduce_fusion.2
  481.3 1.5 fusion.39
  482.8 2.4 fusion.40
  485.2 0.2 copy.30
  485.4 0.1 all_to_all.43
  485.5 0.1 copy.31
  485.6 27.4 %all_to_all.58 = bf16[16,128,72]{1,2,0:T(8,128)(2,1)S(1)} all-to-all(bf16[16,128,72]{1,2,0:T(8,128)(2,1)S(1)} %copy.31), channel_id=1, replica_groups=mesh['frame'=32,'patch'=16] {'patch'}, dimensions={0} | all-to-all | bytes 589824 | tf_op jit(solution)/shard_map/all_to_all | solution.py:92
  513.0 0.7 fusion.14
  513.7 0.0 copy-start.3
  513.8 0.7 copy-done.3
  514.5 0.8 fusion.15
  515.3 0.0 all-gather.5.cloned.1.call-update
  515.3 135.7 %all-gather.5.cloned.1.call-done = bf16[2048,1152]{1,0:T(8,128)(2,1)} async-done(((bf16[128,1152]{1,0:T(8,128)(2,1)}), bf16[2048,1152]{1,0:T(8,128)(2,1)}) %all-gather.5.cloned.1.call-update) | async-done | bytes 4718608 | tf_op jit(solution)/shard_map/all_gather | solution.py:98
  651.0 4.1 convolution_convert_fusion
  655.1 1.3 copy.32
  656.5 33.9 %all_to_all.59 = bf16[1,32,64,216]{3,2,0,1:T(8,128)(2,1)} all-to-all(bf16[1,32,64,216]{3,2,0,1:T(8,128)(2,1)} %bitcast.92), channel_id=1, replica_groups=mesh['frame'=32,'patch'=16] {'frame'}, dimensions={1} | all-to-all | bytes 1769472 | tf_op jit(solution)/shard_map/all_to_all | solution.py:106
  690.4 5.2 reshape_squeeze.7
  695.5 7.0 fusion.21
  702.5 1.0 copy-done.1
  703.5 0.4 copy-done.2
  703.9 2.2 convolution_multiply_fusion
  706.1 2.9 fusion.23
  709.1 2.7 fusion.13
  711.8 0.2 copy.38
  712.0 20.5 %all_to_all.60 = bf16[32,64,72]{2,1,0:T(8,128)(2,1)S(1)} all-to-all(bf16[32,64,72]{2,1,0:T(8,128)(2,1)S(1)} %copy.38), channel_id=1, replica_groups=mesh['frame'=32,'patch'=16] {'frame'}, dimensions={0} | all-to-all | bytes 589824 | tf_op jit(solution)/shard_map/all_to_all | solution.py:112
  732.5 8.9 %copy.69 = bf16[1,2048,72]{2,0,1:T(2,128)(2,1)} copy(bf16[1,2048,72]{2,1,0:T(8,128)(2,1)S(1)} %bitcast.96) | data formatting | bytes 589824 | tf_op jit(solution)/shard_map/all_to_all | solution.py:112
  741.4 0.5 broadcast.60
  741.9 12.6 %reduce.4 = bf16[2048,72]{1,0:T(8,128)(2,1)S(1)} reduce(bf16[2048,1,72]{2,1,0:T(2,128)(2,1)} %bitcast.90, bf16[]{:T(256)} %broadcast.60), dimensions={1}, to_apply=%bitcast.80.reduce_sub_computation | reduce | bytes 589826
  754.5 1.1 reshape.89
  755.6 30.0 %all_to_all.61 = bf16[16,2,4608]{2,1,0:T(2,128)(2,1)S(1)} all-to-all(bf16[16,2,4608]{2,1,0:T(2,128)(2,1)S(1)} %reshape.89), channel_id=1, replica_groups=mesh['frame'=32,'patch'=16] {'patch'}, dimensions={0} | all-to-all | bytes 589824 | tf_op jit(solution)/shard_map/all_to_all | solution.py:111
  785.6 2.8 reshape.90
  788.3 2.3 copy.41
  790.7 0.1 copy.42
  790.7 0.9 copy.43
  (17 shorter events, 0.1 us)
Async XLA Ops:
  7.2 505.9 %copy-start = (bf16[1152,1152]{1,0:T(8,128)(2,1)S(1)}, bf16[1152,1152]{1,0:T(8,128)(2,1)}, u32[]{:S(2)}) copy-start(bf16[1152,1152]{1,0:T(8,128)(2,1)} %param.10) | copy-start | bytes 7962628
  7.2 153.0 %all-gather.3.cloned.1.call-start = ((), (), s32[]{:S(2)}) async-start(), calls=%async_computation.4 | async-start | bytes 5013504 | tf_op jit(solution)/shard_map/all_gather | solution.py:69
  10.3 444.7 %all-reduce.2.cloned.1.call-start = ((), (), s32[]{:S(2)}) async-start(), calls=%async_computation.5 | async-start | bytes 2097152 | tf_op jit(solution)/shard_map/psum | solution.py:16
  169.8 481.2 %all-gather.5.cloned.1.call-start = ((), (), s32[]{:S(2)}) async-start(), calls=%async_computation.6 | async-start | bytes 5013504 | tf_op jit(solution)/shard_map/all_gather | solution.py:98
  170.8 288.4 %copy-start.5 = (bf16[4,512,72]{1,2,0:T(8,128)(2,1)S(1)}, bf16[4,512,72]{1,2,0:T(8,128)(2,1)}, u32[]{:S(2)}) copy-start(bf16[4,512,72]{1,2,0:T(8,128)(2,1)} %custom-call) | copy-start | bytes 884740
  461.8 1.5 copy-start.4
  468.3 1.5 copy-start.4
  474.8 1.5 copy-start.4
  481.3 1.5 copy-start.4
  513.7 0.7 copy-start.3
  702.5 1.0 copy-start.1
  702.5 1.4 copy-start.2
Sparse Core Ops, SparseCore 0:
  11.6 148.5 all-gather.2
  169.9 285.0 all-reduce.1
  515.4 135.4 all-gather.4
where the time goes:
time: 801 us; the launch traced here: 798 us
  waiting for transfers between devices  564 us (70%)
  blocking collectives  112 us (14%)
  local copies, waits for them, and re-layouts  43.2 us (5%)
  matrix products  36.7 us (5%)
  other arithmetic  27.8 us (3%)
  between operations  14.5 us (2%)
    psum x1, waiting for transfers between devices, broadcast(): return lax.psum(jnp.where(mine, x, jnp.zeros_like(x)), axis)  279 us
    all_gather x1, waiting for transfers between devices, per_device(): lax.all_gather(normed, 'patch', axis=0, tiled=True)  149 us
    all_gather x1, waiting for transfers between devices, per_device(): lax.all_gather(temporal_in, 'patch', axis=0, tiled=True)  136 us
    all_to_all x1, blocking collectives, per_device(): lax.all_to_all(grouped_qkv, 'frame', split_axis=1, concat_axis=0, tiled=T...  33.9 us
    all_to_all x1, blocking collectives, per_device(): lax.all_to_all(lax.all_to_all(mixed_heads, 'frame', split_axis=0, concat_...  30 us
    all_to_all x1, blocking collectives, per_device(): lax.all_to_all(outputs, 'patch', split_axis=0, concat_axis=1, tiled=True)  27.4 us
    all_to_all x1, blocking collectives, per_device(): lax.all_to_all(mixed_heads, 'frame', split_axis=0, concat_axis=1, tiled=T...  20.5 us
  transfers between devices with their start and end apart: 3, of which 3 were waited for; matrix products, arithmetic and copies ran while one was open for 1% of the time, Pallas kernels for 0%

commit v1 on v0

v1 whole, which is shorter than its diff:
```python
import functools

import jax
import jax.numpy as jnp
from jax import lax
from jax.experimental import pallas as pl
from jax.experimental.pallas import tpu as pltpu
from jax.sharding import PartitionSpec as P

D = 1152
HEADS = 16
HEAD_DIM = 72
PATCHES = 2048
BLOCK = 128
LANES = 128
CHUNKS = 2
ROWS = BLOCK // CHUNKS
KEY_ROWS = 16
FRAGMENT = D // 8
epsilon = 1e-06
LOG2E = 1.4426950408889634
BF16 = jnp.bfloat16
F32 = jnp.float32


def rms_norm(values):
    values = values.astype(F32)
    return values * lax.rsqrt(jnp.mean(values * values, axis=-1, keepdims=True) + epsilon)


def places():
    patch, frame = lax.axis_index("patch"), lax.axis_index("frame")
    return (
        patch,
        frame,
        lax.div(patch, 4),
        lax.rem(patch, 4),
        lax.div(frame, 8),
        lax.rem(lax.div(frame, 2), 4),
        lax.rem(frame, 2),
    )


def turn(at, by):
    return lax.rem(at + by, 4)


class Links:
    def __init__(self, send, recv):
        self.send, self.recv, self.used, self.open = send, recv, 0, []
        self.patch, self.frame, self.x, self.zh, self.y, self.zl, self.core = places()

    def patch_device(self, dx, dz):
        return (self.frame, turn(self.x, dx) * 4 + turn(self.zh, dz))

    def frame_device(self, dy, dz, dc):
        frame = turn(self.y, dy) * 8 + turn(self.zl, dz) * 2 + lax.rem(self.core + dc, 2)
        return (frame, self.patch)

    def copy(self, src, dst, device):
        made = pltpu.make_async_remote_copy(
            src_ref=src,
            dst_ref=dst,
            send_sem=self.send.at[self.used],
            recv_sem=self.recv.at[self.used],
            device_id=device,
            device_id_type=pl.DeviceIdType.MESH,
        )
        made.start()
        self.used += 1
        self.open.append(made)
        return made

    def finish(self):
        for made in self.open:
            made.wait_send()


def greet(devices):
    barrier = pltpu.get_barrier_semaphore()
    for device in devices:
        pl.semaphore_signal(barrier, inc=1, device_id=device, device_id_type=pl.DeviceIdType.MESH)
    pl.semaphore_wait(barrier, len(devices))


class Gather:
    def __init__(self, links, held, rows):
        self.links, self.held, self.rows = links, held, rows
        self.along_x = {}
        self.last = {}

    def halves(self):
        if self.rows % 32:
            return [(pl.ds(0, self.rows), 0)]
        half = self.rows // 2
        return [(pl.ds(0, half), 0), (pl.ds(half, half), 1)]

    def send_x(self, dz):
        links, held = self.links, self.held
        self.along_x[dz] = (
            links.copy(held.at[dz, 0], held.at[dz, 3], links.patch_device(1, 0)),
            links.copy(held.at[dz, 0], held.at[dz, 1], links.patch_device(3, 0)),
        )

    def begin(self):
        links, held = self.links, self.held
        self.up = links.copy(held.at[0, 0], held.at[3, 0], links.patch_device(0, 1))
        self.down = links.copy(held.at[0, 0], held.at[1, 0], links.patch_device(0, 3))
        self.send_x(0)

    def neighbours(self):
        links, held = self.links, self.held
        self.far = []
        self.up.wait_recv()
        for part, way in self.halves():
            if way == 0:
                self.far.append(
                    links.copy(held.at[3, 0, part], held.at[2, 0, part], links.patch_device(0, 1))
                )
        self.send_x(3)
        self.down.wait_recv()
        for part, way in self.halves():
            if way == 1:
                self.far.append(
                    links.copy(held.at[1, 0, part], held.at[2, 0, part], links.patch_device(0, 3))
                )
        self.send_x(1)

    def opposite(self):
        for made in self.far:
            made.wait_recv()
        self.send_x(2)

    def forward_x(self, dz):
        links, held = self.links, self.held
        up, down = self.along_x[dz]
        self.last[dz] = []
        up.wait_recv()
        for part, way in self.halves():
            if way == 0:
                self.last[dz].append(
                    links.copy(held.at[dz, 3, part], held.at[dz, 2, part], links.patch_device(1, 0))
                )
        down.wait_recv()
        for part, way in self.halves():
            if way == 1:
                self.last[dz].append(
                    links.copy(held.at[dz, 1, part], held.at[dz, 2, part], links.patch_device(3, 0))
                )

    def done_x(self, dz):
        for made in self.last[dz]:
            made.wait_recv()


def with_ones(values):
    lane = lax.broadcasted_iota(jnp.int32, values.shape, 1)
    return jnp.where(lane == HEAD_DIM, jnp.ones_like(values), values)


GATHER_COPIES = 20
FIRST_COPIES = (CHUNKS + 1) * GATHER_COPIES + 7 + 3 + 7 + 12


def project_kernel(
    pick_ref,
    tokens_ref,
    w_ref,
    wt_ref,
    q_ref,
    k_ref,
    v_ref,
    wt4_ref,
    held0,
    held1,
    kheld,
    slices,
    first,
    second,
    kv_out,
    kv_in,
    wt4,
    send,
    recv,
    local_sem,
):
    links = Links(send, recv)
    others = [(dy, dc) for dy in range(4) for dc in range(2) if (dy, dc) != (0, 0)]
    greet(
        [links.patch_device(dx, dz) for dx, dz in ((1, 0), (3, 0), (0, 1), (0, 2), (0, 3))]
        + [links.frame_device(dy, 0, dc) for dy, dc in others]
        + [links.frame_device(0, dz, 0) for dz in (1, 2, 3)]
    )
    held = (held0, held1)
    normed = rms_norm(tokens_ref[...]).astype(BF16)
    for c in range(CHUNKS):
        held[c][0, 0] = normed[c * ROWS : (c + 1) * ROWS]
    for g in range(8):
        slices[g] = normed[g * KEY_ROWS : (g + 1) * KEY_ROWS]
    picks = []
    for dy, dc in others:
        there = turn(links.y, dy) * 2 + lax.rem(links.core + dc, 2)
        slot = (4 - dy) % 4 * 2 + dc
        picks.append(
            links.copy(slices.at[there], first.at[slot], links.frame_device(dy, 0, dc))
        )
    gathers = [Gather(links, held[c], ROWS) for c in range(CHUNKS)]
    gathers[0].begin()
    gathers[1].begin()
    part = pl.ds(pl.multiple_of((links.core * 4 + links.y) * FRAGMENT, 16), FRAGMENT)
    own = pltpu.make_async_copy(wt_ref.at[part], wt4.at[links.zh, part], local_sem)
    own.start()
    own.wait()
    wt_z = [
        links.copy(wt4.at[links.zh, part], wt4.at[links.zh, part], links.patch_device(0, dz))
        for dz in (1, 2, 3)
    ]
    here = links.y * 2 + links.core
    first[0] = slices[here]
    for made in picks:
        made.wait_recv()
    second[0] = first[pick_ref[0]]
    picks = [
        links.copy(second.at[0], second.at[4 - dz], links.frame_device(0, dz, 0))
        for dz in (1, 2, 3)
    ]
    for made in picks:
        made.wait_recv()
    kheld[0, 0] = second[pick_ref[1]]
    keys = Gather(links, kheld, KEY_ROWS)
    keys.begin()
    gathers[0].neighbours()
    keys.neighbours()
    gathers[1].neighbours()
    for made in wt_z:
        made.wait_recv()
    wt_y = [
        links.copy(wt4.at[:, part], wt4.at[:, part], links.frame_device(dy, 0, 0))
        for dy in (1, 3, 2)
    ]
    gathers[0].forward_x(0)
    gathers[1].forward_x(0)
    keys.forward_x(0)
    gathers[0].opposite()
    keys.opposite()
    gathers[1].opposite()

    def store(block, c, dz):
        out = jnp.dot(block, w_ref[...], preferred_element_type=F32)
        for dx in range(4):
            patch = turn(links.x, dx) * 4 + turn(links.zh, dz)
            at = pl.ds(pl.multiple_of(patch * BLOCK + c * ROWS, ROWS), ROWS)
            rows = out[dx * ROWS : (dx + 1) * ROWS]
            q_ref[at, :] = (rows[:, :LANES] * (HEAD_DIM**-0.5 * LOG2E)).astype(BF16)
            k_ref[at, :] = rows[:, LANES : 2 * LANES].astype(BF16)
            v_ref[at, :] = with_ones(rows[:, 2 * LANES :]).astype(BF16)

    def finish(dz):
        for c in range(CHUNKS):
            gathers[c].done_x(dz)
            store(held[c][dz].reshape(4 * ROWS, D), c, dz)

    for dz in (3, 1):
        for one in (gathers[0], keys, gathers[1]):
            one.forward_x(dz)
    keys.forward_x(2)
    finish(0)
    finish(3)
    for made in wt_y:
        made.wait_recv()
    half = pl.ds(pl.multiple_of(links.core * 4 * FRAGMENT, 16), 4 * FRAGMENT)
    wt_c = links.copy(wt4.at[:, half], wt4.at[:, half], links.frame_device(0, 0, 1))
    for dz in range(4):
        keys.done_x(dz)
    kv_out[...] = jnp.dot(
        kheld[...].reshape(16 * KEY_ROWS, D), w_ref[:, LANES:], preferred_element_type=F32
    ).astype(BF16)
    kv = [
        links.copy(kv_out, kv_in.at[(4 - dy) % 4 * 2 + dc], links.frame_device(dy, 0, dc))
        for dy, dc in others
    ]
    finish(1)
    for one in gathers:
        one.forward_x(2)
    finish(2)
    kv_in[0] = kv_out[...]
    for made in kv:
        made.wait_recv()
    for g in range(8):
        at = pl.ds(PATCHES + g * 16 * KEY_ROWS, 16 * KEY_ROWS)
        k_ref[at, :] = kv_in[g, :, :LANES]
        v_ref[at, :] = with_ones(kv_in[g, :, LANES:].astype(F32)).astype(BF16)
    wt_c.wait_recv()
    wt4_ref[...] = wt4[...]
    links.finish()


def project(pick, tokens, w, wt):
    vmem = pl.BlockSpec(memory_space=pltpu.VMEM)
    columns = wt.shape[1]
    return pl.pallas_call(
        project_kernel,
        out_shape=[
            jax.ShapeDtypeStruct((PATCHES, LANES), BF16),
            jax.ShapeDtypeStruct((2 * PATCHES, LANES), BF16),
            jax.ShapeDtypeStruct((2 * PATCHES, LANES), BF16),
            jax.ShapeDtypeStruct((4, D, columns), BF16),
        ],
        in_specs=[pl.BlockSpec(memory_space=pltpu.SMEM), vmem, vmem, vmem],
        out_specs=[vmem] * 4,
        scratch_shapes=[
            pltpu.VMEM((4, 4, ROWS, D), BF16),
            pltpu.VMEM((4, 4, ROWS, D), BF16),
            pltpu.VMEM((4, 4, KEY_ROWS, D), BF16),
            pltpu.VMEM((8, KEY_ROWS, D), BF16),
            pltpu.VMEM((8, KEY_ROWS, D), BF16),
            pltpu.VMEM((4, KEY_ROWS, D), BF16),
            pltpu.VMEM((16 * KEY_ROWS, 2 * LANES), BF16),
            pltpu.VMEM((8, 16 * KEY_ROWS, 2 * LANES), BF16),
            pltpu.VMEM((4, D, columns), BF16),
            pltpu.SemaphoreType.DMA((FIRST_COPIES,)),
            pltpu.SemaphoreType.DMA((FIRST_COPIES,)),
            pltpu.SemaphoreType.DMA,
        ],
        compiler_params=pltpu.CompilerParams(
            collective_id=1, has_side_effects=True, vmem_limit_bytes=48 * 2**20
        ),
        name="project",
    )(pick, tokens, w, wt)


Q_ROWS = 256
KEY_STEP = 2048


def attend_kernel(q_ref, k_ref, v_ref, wt4_ref, o_ref, wt_ref, kt, send, recv, local_sem):
    links = Links(send, recv)
    greet([links.patch_device(1, 0), links.patch_device(3, 0), links.frame_device(0, 0, 1)])
    x = links.x
    mine = pl.ds(pl.multiple_of(links.core * (D // 2), 16), D // 2)

    def group(at):
        return pl.ds(at * 4, 4)

    up = links.copy(wt4_ref.at[:, mine], wt_ref.at[group(x), mine], links.patch_device(1, 0))
    down = links.copy(wt4_ref.at[:, mine], wt_ref.at[group(x), mine], links.patch_device(3, 0))
    own = pltpu.make_async_copy(wt4_ref, wt_ref.at[group(x)], local_sem)
    own.start()
    for j in range(2 * PATCHES // 512):
        kt[:, j * 512 : (j + 1) * 512] = k_ref[j * 512 : (j + 1) * 512, :].T

    def rows_of(i):
        q = q_ref[pl.ds(pl.multiple_of(i * Q_ROWS, Q_ROWS), Q_ROWS), :]
        total = largest = None
        for j in range(2 * PATCHES // KEY_STEP):
            keys = slice(j * KEY_STEP, (j + 1) * KEY_STEP)
            scores = jnp.dot(q, kt[:, keys], preferred_element_type=F32)
            new = jnp.max(scores, axis=-1, keepdims=True)
            if j:
                new = jnp.maximum(largest, new)
            weights = jnp.exp2(scores - new).astype(BF16)
            part = jnp.dot(weights, v_ref[keys, :], preferred_element_type=F32)
            total = part if j == 0 else total * jnp.exp2(largest - new) + part
            largest = new
        out = total / total[:, HEAD_DIM : HEAD_DIM + 1]
        turned = out.T
        for b in range(Q_ROWS // BLOCK):
            o_ref[i * (Q_ROWS // BLOCK) + b] = turned[:HEAD_DIM, b * BLOCK : (b + 1) * BLOCK].astype(BF16)

    def loop(first, last):
        pl.loop(first, last)(rows_of)

    steps = PATCHES // Q_ROWS
    loop(0, steps // 2)
    own.wait()
    quarter = D // 4
    up.wait_recv()
    lower = pl.ds(pl.multiple_of(links.core * (D // 2), 16), quarter)
    upper = pl.ds(pl.multiple_of(links.core * (D // 2) + quarter, 16), quarter)
    left, right = group(turn(x, 3)), group(turn(x, 1))
    far = [links.copy(wt_ref.at[left, lower], wt_ref.at[left, lower], links.patch_device(1, 0))]
    other = links.frame_device(0, 0, 1)
    cross = [links.copy(wt_ref.at[left, mine], wt_ref.at[left, mine], other)]
    down.wait_recv()
    far.append(links.copy(wt_ref.at[right, upper], wt_ref.at[right, upper], links.patch_device(3, 0)))
    cross.append(links.copy(wt_ref.at[right, mine], wt_ref.at[right, mine], other))
    loop(steps // 2, steps)
    for made in far:
        made.wait_recv()
    opposite = group(turn(x, 2))
    cross.append(links.copy(wt_ref.at[opposite, mine], wt_ref.at[opposite, mine], other))
    for made in cross:
        made.wait_recv()
    links.finish()


def attend(q, k, v, wt4):
    vmem = pl.BlockSpec(memory_space=pltpu.VMEM)
    anywhere = pl.BlockSpec(memory_space=pl.ANY)
    columns = wt4.shape[2]
    return pl.pallas_call(
        attend_kernel,
        out_shape=[
            jax.ShapeDtypeStruct((HEADS, HEAD_DIM, BLOCK), BF16),
            jax.ShapeDtypeStruct((HEADS, D, columns), BF16),
        ],
        in_specs=[vmem, vmem, vmem, anywhere],
        out_specs=[vmem, anywhere],
        scratch_shapes=[
            pltpu.VMEM((LANES, 2 * PATCHES), BF16),
            pltpu.SemaphoreType.DMA((7,)),
            pltpu.SemaphoreType.DMA((7,)),
            pltpu.SemaphoreType.DMA,
        ],
        compiler_params=pltpu.CompilerParams(
            collective_id=2, has_side_effects=True, vmem_limit_bytes=48 * 2**20
        ),
        name="attend",
    )(q, k, v, wt4)


def temporal_kernel(x_ref, wt_ref, o_ref, turned):
    x = x_ref[...]
    row = lax.broadcasted_iota(jnp.int32, (BLOCK, BLOCK), 0)
    column = lax.broadcasted_iota(jnp.int32, (BLOCK, BLOCK), 1)
    same = (row & 3) == (column & 3)
    for h in range(HEADS):
        qkv = jnp.dot(x, wt_ref[h], preferred_element_type=F32).astype(BF16)
        q, k, v = (qkv[:, i * HEAD_DIM : (i + 1) * HEAD_DIM] for i in range(3))
        scores = lax.dot_general(
            q, k, (((1,), (1,)), ((), ())), preferred_element_type=F32
        ) * (HEAD_DIM**-0.5)
        scores = jnp.where(same, scores, -jnp.inf)
        exponent = jnp.exp(scores - jnp.max(scores, axis=-1, keepdims=True))
        weights = (exponent / jnp.sum(exponent, axis=-1, keepdims=True)).astype(BF16)
        out = jnp.dot(weights, v, preferred_element_type=F32)
        turned[h * HEAD_DIM : (h + 1) * HEAD_DIM, :] = out.T
    o_ref[...] = turned[...].T.astype(BF16)


def temporal_attend(x, wt):
    vmem = pl.BlockSpec(memory_space=pltpu.VMEM)
    return pl.pallas_call(
        temporal_kernel,
        out_shape=jax.ShapeDtypeStruct((BLOCK, D), BF16),
        in_specs=[vmem, vmem],
        out_specs=vmem,
        scratch_shapes=[pltpu.VMEM((D, BLOCK), F32)],
        compiler_params=pltpu.CompilerParams(vmem_limit_bytes=48 * 2**20),
        name="temporal_attend",
    )(x, wt)


def per_device(tokens, key_frame, qkv_spatial, out_spatial, qkv_temporal):
    frame = lax.axis_index("frame")
    key = key_frame[0].astype(jnp.int32)
    y, zl, core = frame // 8, (frame // 2) % 4, frame % 2
    pick = jnp.stack(
        [(key // 8 - y) % 4 * 2 + (key % 2 - core) % 2, (key // 2 % 4 - zl) % 4]
    ).astype(jnp.int32)
    w = qkv_spatial.reshape(D, 3, HEAD_DIM)
    w = jnp.pad(w, ((0, 0), (0, 0), (0, LANES - HEAD_DIM))).reshape(D, 3 * LANES)
    q, k, v, wt4 = project(pick, tokens[0], w, qkv_temporal)
    heads, wt = attend(q, k, v, wt4)
    heads = lax.all_to_all(heads, "patch", split_axis=0, concat_axis=0, tiled=True)
    spatial = lax.dot_general(
        heads.reshape(D, BLOCK), out_spatial, (((0,), (0,)), ((), ())), preferred_element_type=F32
    ).astype(BF16)
    temporal_in = rms_norm(spatial).astype(BF16)
    rows = lax.all_to_all(
        temporal_in.reshape(32, 4, D), "frame", split_axis=0, concat_axis=0, tiled=True
    )
    mixed = temporal_attend(rows.reshape(BLOCK, D), wt)
    temporal = lax.all_to_all(
        mixed.reshape(32, 4, D), "frame", split_axis=0, concat_axis=0, tiled=True
    )
    return (spatial[None], temporal.reshape(1, BLOCK, D))


def solution(mesh):
    return jax.shard_map(
        per_device,
        mesh=mesh,
        in_specs=(P("frame", "patch", None), P(), P(None, "patch"), P(), P(None, "patch")),
        out_specs=(P("frame", "patch", None), P("frame", "patch", None)),
        check_vma=False,
    )
```

time: 801 us -> 254 us (0.32)
  waiting for transfers between devices: 564 us -> 0 us
  Pallas kernels: 0 us -> 173 us
  blocking collectives: 112 us -> 66.7 us
  matrix products: 36.7 us -> 0.71 us
  local copies, waits for them, and re-layouts: 43.2 us -> 10.6 us
  other arithmetic: 27.8 us -> 0.2 us
  between operations: 14.5 us -> 1.69 us
    all_gather x2 -> x0, waiting for transfers between devices: 285 us -> none  [the longest x1 149 us: per_device(): lax.all_gather(normed, 'patch', axis=0, tiled=True)]
    psum x1 -> x0, waiting for transfers between devices: 279 us -> none  [broadcast(): return lax.psum(jnp.where(mine, x, jnp.zeros_like(x)), axis)]
    pallas_call x0 -> x3, Pallas kernels: none -> 173 us  [the longest x1 112 us: project(): pl.pallas_call(project_kernel, out_shape=[jax.ShapeDtypeStruct((PATCHES,...]
    all_to_all x4 -> x3, blocking collectives: 112 us -> 66.7 us  [the longest x1 27.3 us: per_device(): lax.all_to_all(heads, 'patch', split_axis=0, concat_axis=0, tiled=True)]
    dot_general x13 -> x1, matrix products: 33.8 us -> 0.71 us  [per_device(): lax.dot_general(heads.reshape(D, BLOCK), out_spatial, (((0,), (0,)), ((),...]
    unnamed x1 -> x0, other arithmetic: 12.6 us -> none
    all_to_all x5 -> x0, local copies, waits for them, and re-layouts: 11.5 us -> none  [the longest x1 8.91 us: per_device(): lax.all_to_all(mixed_heads, 'frame', split_axis=0, concat_axis=1, tiled=T...]
    slice x4 -> x0, local copies, waits for them, and re-layouts: 9.99 us -> none  [the longest x1 6.97 us: temporal_attend(): split_qkv[:, :, :, 0]]
  transfers between devices with their start and end apart: 3 -> 0, of which waited for: 3 -> 0; matrix products, arithmetic and copies ran while one was open for 1% -> 0% of each run, Pallas kernels for 0% -> 0%
where the time goes in v1:
time: 254 us; the launch traced here: 253 us
  Pallas kernels  173 us (68%)
  blocking collectives  66.7 us (26%)
  local copies, waits for them, and re-layouts  10.6 us (4%)
    pallas_call x1, Pallas kernels, project(): pl.pallas_call(project_kernel, out_shape=[jax.ShapeDtypeStruct((PATCHES,...  112 us
    pallas_call x1, Pallas kernels, attend(): pl.pallas_call(attend_kernel, out_shape=[jax.ShapeDtypeStruct((HEADS, HEA...  46.6 us
    all_to_all x1, blocking collectives, per_device(): lax.all_to_all(heads, 'patch', split_axis=0, concat_axis=0, tiled=True)  27.3 us
    all_to_all x1, blocking collectives, per_device(): lax.all_to_all(temporal_in.reshape(32, 4, D), 'frame', split_axis=0, conc...  24 us
    all_to_all x1, blocking collectives, per_device(): lax.all_to_all(mixed.reshape(32, 4, D), 'frame', split_axis=0, concat_axi...  15.4 us
    pallas_call x1, Pallas kernels, temporal_attend(): pl.pallas_call(temporal_kernel, out_shape=jax.ShapeDtypeStruct((BLOCK, D)...  14.9 us
    unnamed x11, local copies, waits for them, and re-layouts  5.82 us

profile of v1, /device:TPU:1, one launch (start us, length us, event | category | flops | bytes accessed | tf_op | source)
XLA Modules:
  0.0 253.3 jit_solution(5150678605253680768)
XLA Ops:
  0.6 0.0 copy-start
  1.6 2.1 copy.10.wt_ref
  3.7 2.0 pad.4
  5.7 1.7 copy.9.w_ref
  7.5 0.1 pad_add_fusion.pick_ref
  7.6 0.0 copy-start.2
  7.6 1.1 copy-done.2
  8.6 0.0 copy-start.3
  8.6 1.0 copy-done.3
  9.6 111.9 %project.1 = (bf16[2048,128]{1,0:T(8,128)(2,1)S(1)}, bf16[4096,128]{1,0:T(8,128)(2,1)S(1)}, bf16[4096,128]{1,0:T(8,128)(2,1)S(1)}, bf16[4,1152,216]{2,1,0:T(8,128)(2,1)}) custom-call(s32[2]{0:T(128)S(1)} %pad_add_fusion.pick_ref, bf16[128,1152]{1,0:T(8,128)(2,1)S(1)} %bitcast.14, bf16[1152,384]{1,0:T(8,128)(2,1)S(1)} %copy.9.w_ref, ...), custom_call_target="tpu_custom_call" | custom-call | tf_op jit(solution)/shard_map/project/pallas_call | solution.py:301
  121.5 0.0 copy-start.1
  121.5 1.7 copy-done.1
  123.2 46.6 %attend.1 = (bf16[16,72,128]{2,1,0:T(8,128)(2,1)S(1)}, bf16[16,1152,216]{2,1,0:T(8,128)(2,1)}) custom-call(bf16[2048,128]{1,0:T(8,128)(2,1)S(1)} %get-tuple-element.8.q_ref, bf16[4096,128]{1,0:T(8,128)(2,1)S(1)} %get-tuple-element.9.k_ref, bf16[4096,128]{1,0:T(8,128)(2,1)S(1)} %get-tuple-element.10.v_ref, bf16[4,1152,216]{2,1,0:T(8,128)(2,1)S(1)} %copy-done.1), custom_call_target="tpu_custom_call" | custom-call | tf_op jit(solution)/shard_map/attend/pallas_call | solution.py:401
  169.8 27.3 %all_to_all.15 = bf16[16,72,128]{2,1,0:T(8,128)(2,1)S(1)} all-to-all(bf16[16,72,128]{2,1,0:T(8,128)(2,1)S(1)} %get-tuple-element.12), channel_id=1, replica_groups=mesh['frame'=32,'patch'=16] {'patch'}, dimensions={0} | all-to-all | bytes 589824 | tf_op jit(solution)/shard_map/all_to_all | solution.py:465
  197.1 0.0 copy-done
  197.1 0.7 fusion
  197.8 0.0 copy-start.4
  197.8 0.1 fusion.1
  198.0 0.1 reshape.36
  198.1 24.0 %all_to_all.16 = bf16[32,4,1152]{2,1,0:T(4,128)(2,1)S(1)} all-to-all(bf16[32,4,1152]{2,1,0:T(4,128)(2,1)S(1)} %reshape.36), channel_id=1, replica_groups=mesh['frame'=32,'patch'=16] {'frame'}, dimensions={0} | all-to-all | bytes 589824 | tf_op jit(solution)/shard_map/all_to_all | solution.py:470
  222.1 0.1 reshape.37.x_ref
  222.1 14.9 %temporal_attend.1 = bf16[128,1152]{1,0:T(8,128)(2,1)S(1)} custom-call(bf16[128,1152]{1,0:T(8,128)(2,1)S(1)} %reshape.37.x_ref, bf16[16,1152,216]{2,1,0:T(8,128)(2,1)} %get-tuple-element.13.wt_ref), custom_call_target="tpu_custom_call" | custom-call | tf_op jit(solution)/shard_map/temporal_attend/pallas_call | solution.py:443
  237.0 0.0 copy-done.4
  237.1 0.1 reshape.38
  237.1 15.4 %all_to_all.17 = bf16[32,4,1152]{2,1,0:T(4,128)(2,1)S(1)} all-to-all(bf16[32,4,1152]{2,1,0:T(4,128)(2,1)S(1)} %reshape.38), channel_id=1, replica_groups=mesh['frame'=32,'patch'=16] {'frame'}, dimensions={0} | all-to-all | bytes 589824 | tf_op jit(solution)/shard_map/all_to_all | solution.py:474
  252.5 0.8 reshape.39
  (1 shorter events, 0.0 us)
Async XLA Ops:
  0.6 196.5 %copy-start = (bf16[1152,1152]{1,0:T(8,128)(2,1)S(1)}, bf16[1152,1152]{1,0:T(8,128)(2,1)}, u32[]{:S(2)}) copy-start(bf16[1152,1152]{1,0:T(8,128)(2,1)} %param.8) | copy-start | bytes 7962628
  7.6 1.1 copy-start.2
  8.6 1.0 copy-start.3
  121.5 1.7 copy-start.1
  197.8 39.2 %copy-start.4 = (bf16[128,1152]{1,0:T(8,128)(2,1)}, bf16[128,1152]{1,0:T(8,128)(2,1)S(1)}, u32[]{:S(2)}) copy-start(bf16[128,1152]{1,0:T(8,128)(2,1)S(1)} %get-tuple-element.15) | copy-start | bytes 884740

commit v2 on v1

v2 whole, which is shorter than its diff:
```python
import functools

import jax
import jax.numpy as jnp
from jax import lax
from jax.experimental import pallas as pl
from jax.experimental.pallas import tpu as pltpu
from jax.sharding import PartitionSpec as P

D = 1152
HEADS = 16
HEAD_DIM = 72
PATCHES = 2048
BLOCK = 128
LANES = 128
CHUNKS = 2
ROWS = BLOCK // CHUNKS
KEY_ROWS = 16
FRAGMENT = D // 8
epsilon = 1e-06
LOG2E = 1.4426950408889634
BF16 = jnp.bfloat16
F32 = jnp.float32


def rms_norm(values):
    values = values.astype(F32)
    return values * lax.rsqrt(jnp.mean(values * values, axis=-1, keepdims=True) + epsilon)


def places():
    patch, frame = lax.axis_index("patch"), lax.axis_index("frame")
    return (
        patch,
        frame,
        lax.div(patch, 4),
        lax.rem(patch, 4),
        lax.div(frame, 8),
        lax.rem(lax.div(frame, 2), 4),
        lax.rem(frame, 2),
    )


def turn(at, by):
    return lax.rem(at + by, 4)


class Links:
    def __init__(self, send, recv):
        self.send, self.recv, self.used, self.open = send, recv, 0, []
        self.patch, self.frame, self.x, self.zh, self.y, self.zl, self.core = places()

    def patch_device(self, dx, dz):
        return (self.frame, turn(self.x, dx) * 4 + turn(self.zh, dz))

    def frame_device(self, dy, dz, dc):
        frame = turn(self.y, dy) * 8 + turn(self.zl, dz) * 2 + lax.rem(self.core + dc, 2)
        return (frame, self.patch)

    def copy(self, src, dst, device):
        made = pltpu.make_async_remote_copy(
            src_ref=src,
            dst_ref=dst,
            send_sem=self.send.at[self.used],
            recv_sem=self.recv.at[self.used],
            device_id=device,
            device_id_type=pl.DeviceIdType.MESH,
        )
        made.start()
        self.used += 1
        self.open.append(made)
        return made

    def finish(self):
        for made in self.open:
            made.wait_send()


def greet(devices):
    barrier = pltpu.get_barrier_semaphore()
    for device in devices:
        pl.semaphore_signal(barrier, inc=1, device_id=device, device_id_type=pl.DeviceIdType.MESH)
    pl.semaphore_wait(barrier, len(devices))


class Gather:
    def __init__(self, links, held, rows):
        self.links, self.held, self.rows = links, held, rows
        self.along_x = {}
        self.last = {}

    def halves(self):
        if self.rows % 32:
            return [(pl.ds(0, self.rows), 0)]
        half = self.rows // 2
        return [(pl.ds(0, half), 0), (pl.ds(half, half), 1)]

    def send_x(self, dz):
        links, held = self.links, self.held
        self.along_x[dz] = (
            links.copy(held.at[dz, 0], held.at[dz, 3], links.patch_device(1, 0)),
            links.copy(held.at[dz, 0], held.at[dz, 1], links.patch_device(3, 0)),
        )

    def begin_z(self):
        links, held = self.links, self.held
        self.up = links.copy(held.at[0, 0], held.at[3, 0], links.patch_device(0, 1))
        self.down = links.copy(held.at[0, 0], held.at[1, 0], links.patch_device(0, 3))

    def neighbours(self):
        links, held = self.links, self.held
        self.far = []
        self.up.wait_recv()
        for part, way in self.halves():
            if way == 0:
                self.far.append(
                    links.copy(held.at[3, 0, part], held.at[2, 0, part], links.patch_device(0, 1))
                )
        self.send_x(3)
        self.down.wait_recv()
        for part, way in self.halves():
            if way == 1:
                self.far.append(
                    links.copy(held.at[1, 0, part], held.at[2, 0, part], links.patch_device(0, 3))
                )
        self.send_x(1)

    def opposite(self):
        for made in self.far:
            made.wait_recv()
        self.send_x(2)

    def forward_x(self, dz):
        links, held = self.links, self.held
        up, down = self.along_x[dz]
        self.last[dz] = []
        up.wait_recv()
        for part, way in self.halves():
            if way == 0:
                self.last[dz].append(
                    links.copy(held.at[dz, 3, part], held.at[dz, 2, part], links.patch_device(1, 0))
                )
        down.wait_recv()
        for part, way in self.halves():
            if way == 1:
                self.last[dz].append(
                    links.copy(held.at[dz, 1, part], held.at[dz, 2, part], links.patch_device(3, 0))
                )

    def done_x(self, dz):
        for made in self.last[dz]:
            made.wait_recv()


def with_ones(values):
    lane = lax.broadcasted_iota(jnp.int32, values.shape, 1)
    return jnp.where(lane == HEAD_DIM, jnp.ones_like(values), values)


GATHER_COPIES = 20
COPIES = (CHUNKS + 1) * GATHER_COPIES + 7 + 3 + 7 + 3 + 6 + 6 + 8 + 15
SPLIT = 80
GROUP = 512


def spatial_kernel(
    pick_ref,
    tokens_ref,
    w_ref,
    wt_ref,
    out_w_ref,
    spatial_ref,
    normed_ref,
    wt,
    held0,
    held1,
    kheld,
    slices,
    first,
    second,
    w,
    q_s,
    kt,
    v_s,
    kv_out,
    kv_in,
    total_s,
    largest_s,
    out_s,
    heads,
    send,
    recv,
    local_sem,
):
    links = Links(send, recv)
    x, y, core = links.x, links.y, links.core
    others = [(dy, dc) for dy in range(4) for dc in range(2) if (dy, dc) != (0, 0)]
    turns = [(dz, dx) for dz in (0, 3, 1, 2) for dx in range(4)]
    greet(
        [links.patch_device(dx, dz) for dz, dx in turns if (dz, dx) != (0, 0)]
        + [links.frame_device(dy, 0, dc) for dy, dc in others]
        + [links.frame_device(0, dz, 0) for dz in (1, 2, 3)]
    )
    held = (held0, held1)
    normed = rms_norm(tokens_ref[...]).astype(BF16)
    for g in range(8):
        slices[g] = normed[g * KEY_ROWS : (g + 1) * KEY_ROWS]
    picks = []
    for dy, dc in others:
        there = turn(y, dy) * 2 + lax.rem(core + dc, 2)
        slot = (4 - dy) % 4 * 2 + dc
        picks.append(
            links.copy(slices.at[there], first.at[slot], links.frame_device(dy, 0, dc))
        )
    for c in range(CHUNKS):
        held[c][0, 0] = normed[c * ROWS : (c + 1) * ROWS]
    gathers = [Gather(links, held[c], ROWS) for c in range(CHUNKS)]
    for one in gathers:
        one.send_x(0)
    mine = wt_ref.at[pl.ds(pl.multiple_of((core * 4 + y) * FRAGMENT, 16), FRAGMENT)]
    place = wt.at[links.patch, core, y]
    own = pltpu.make_async_copy(mine, place, local_sem)
    own.start()
    first[0] = slices[y * 2 + core]
    for made in picks:
        made.wait_recv()
    second[0] = first[pick_ref[0]]
    picks = [
        links.copy(second.at[0], second.at[4 - dz], links.frame_device(0, dz, 0))
        for dz in (1, 2, 3)
    ]
    for one in gathers:
        one.begin_z()
    wt_up = links.copy(mine, place, links.patch_device(0, 1))
    wt_down = links.copy(mine, place, links.patch_device(0, 3))
    w[...] = jnp.zeros_like(w)
    for i in range(3):
        w[:, i * LANES : i * LANES + HEAD_DIM] = w_ref[:, i * HEAD_DIM : (i + 1) * HEAD_DIM]
    for made in picks:
        made.wait_recv()
    kheld[0, 0] = second[pick_ref[1]]
    keys = Gather(links, kheld, KEY_ROWS)
    keys.send_x(0)
    keys.begin_z()
    for one in gathers:
        one.forward_x(0)
    for one in (gathers[0], gathers[1], keys):
        one.neighbours()
    wt_up.wait_recv()
    below = wt.at[x * 4 + turn(links.zh, 3), core, y]
    wt_far = links.copy(below, below, links.patch_device(0, 1))
    keys.forward_x(0)

    def finish(dz):
        for c in range(CHUNKS):
            gathers[c].done_x(dz)
            out = jnp.dot(
                held[c][dz].reshape(4 * ROWS, D), w[...], preferred_element_type=F32
            )
            q = (out[:, :LANES] * (HEAD_DIM**-0.5 * LOG2E)).astype(BF16)
            for dx in range(4):
                at = (dz * 4 + dx) * BLOCK + c * ROWS
                q_s[at : at + ROWS, :] = q[dx * ROWS : (dx + 1) * ROWS]
            at = (dz * CHUNKS + c) * 4 * ROWS
            kt[:, at : at + 4 * ROWS] = out[:, LANES : 2 * LANES].T.astype(BF16)
            v_s[at : at + 4 * ROWS, :] = with_ones(out[:, 2 * LANES :]).astype(BF16)

    finish(0)
    for dz in (3, 1):
        for one in (gathers[0], gathers[1], keys):
            one.forward_x(dz)
    for one in (gathers[0], gathers[1], keys):
        one.opposite()
    own.wait()
    wt_down.wait_recv()
    wt_far.wait_recv()
    group = pl.ds(x * 4, 4)
    upper, lower = pl.ds(0, SPLIT), pl.ds(SPLIT, FRAGMENT - SPLIT)
    by_y, by_x = wt.at[group, core, y, upper], wt.at[group, core, y, lower]
    steps = []
    for d in (1, 3, 2):
        steps.append(links.copy(by_y, by_y, links.frame_device(d, 0, 0)))
        steps.append(links.copy(by_x, by_x, links.patch_device(d, 0)))
    finish(3)
    finish(1)
    for one in (gathers[0], gathers[1], keys):
        one.forward_x(2)
    for dz in range(4):
        keys.done_x(dz)
    kv_out[...] = jnp.dot(
        kheld[...].reshape(16 * KEY_ROWS, D), w[:, LANES:], preferred_element_type=F32
    ).astype(BF16)
    kv = [
        links.copy(kv_out, kv_in.at[(4 - dy) % 4 * 2 + dc], links.frame_device(dy, 0, dc))
        for dy, dc in others
    ]
    finish(2)
    for made in steps:
        made.wait_recv()
    def along_x(dx, rows=upper, half=slice(0, 4)):
        return wt.at[pl.ds(turn(x, dx) * 4, 4), core, pl.ds(half.start, half.stop - half.start), rows]

    def along_y(dy, half=slice(0, 16)):
        return wt.at[pl.ds(half.start, half.stop - half.start), core, turn(y, dy), lower]

    def pass_on(piece, device):
        return links.copy(piece, piece, device)

    twin = links.frame_device(0, 0, 1)
    x_up = pass_on(along_x(0), links.patch_device(1, 0))
    x_down = pass_on(along_x(0), links.patch_device(3, 0))
    y_up = pass_on(along_y(0), links.frame_device(1, 0, 0))
    y_down = pass_on(along_y(0), links.frame_device(3, 0, 0))
    cross = [pass_on(along_x(0), twin), pass_on(along_y(0), twin)]

    def scores_of(g, keys):
        q = q_s[g * GROUP : (g + 1) * GROUP, :]
        scores = jnp.dot(q, kt[:, keys], preferred_element_type=F32)
        return scores, jnp.max(scores, axis=-1, keepdims=True)

    for g in range(4):
        scores, largest = scores_of(g, slice(0, PATCHES))
        weights = jnp.exp2(scores - largest).astype(BF16)
        total_s[g] = jnp.dot(weights, v_s[:PATCHES, :], preferred_element_type=F32)
        largest_s[g] = jnp.broadcast_to(largest, (GROUP, LANES))
    kv_in[0] = kv_out[...]
    for made in kv:
        made.wait_recv()
    for g in range(8):
        at = PATCHES + g * 16 * KEY_ROWS
        kt[:, at : at + 16 * KEY_ROWS] = kv_in[g, :, :LANES].T
        v_s[at : at + 16 * KEY_ROWS, :] = with_ones(kv_in[g, :, LANES:].astype(F32)).astype(BF16)
    sent = []
    for i, g in enumerate((2, 3, 1, 0)):
        scores, new = scores_of(g, slice(PATCHES, 2 * PATCHES))
        largest = largest_s[g][:, :1]
        new = jnp.maximum(largest, new)
        weights = jnp.exp2(scores - new).astype(BF16)
        total = total_s[g] * jnp.exp2(largest - new) + jnp.dot(
            weights, v_s[PATCHES:, :], preferred_element_type=F32
        )
        turned = (total / total[:, HEAD_DIM : HEAD_DIM + 1]).T
        for dx in (2, 1, 3, 0):
            block = turned[:HEAD_DIM, dx * BLOCK : (dx + 1) * BLOCK].astype(BF16)
            if (g, dx) == (0, 0):
                heads[links.patch] = block
            else:
                out_s[g * 4 + dx] = block
                sent.append(
                    links.copy(
                        out_s.at[g * 4 + dx], heads.at[links.patch], links.patch_device(dx, g)
                    )
                )
        if i == 1:
            x_up.wait_recv()
            far = [pass_on(along_x(3, half=slice(0, 2)), links.patch_device(1, 0))]
            cross.append(pass_on(along_x(3), twin))
            y_up.wait_recv()
            far.append(pass_on(along_y(3, slice(0, 8)), links.frame_device(1, 0, 0)))
            cross.append(pass_on(along_y(3), twin))
            x_down.wait_recv()
            far.append(pass_on(along_x(1, half=slice(2, 4)), links.patch_device(3, 0)))
            cross.append(pass_on(along_x(1), twin))
            y_down.wait_recv()
            far.append(pass_on(along_y(1, slice(8, 16)), links.frame_device(3, 0, 0)))
            cross.append(pass_on(along_y(1), twin))
    for made in sent:
        made.wait_recv()
    rows = heads[...].reshape(D, BLOCK).T
    spatial = jnp.dot(rows, out_w_ref[...], preferred_element_type=F32).astype(BF16)
    spatial_ref[...] = spatial
    normed_ref[...] = rms_norm(spatial).astype(BF16)
    for made in far:
        made.wait_recv()
    cross.append(pass_on(along_x(2), twin))
    cross.append(pass_on(along_y(2), twin))
    for made in cross:
        made.wait_recv()
    links.finish()


def spatial_branch(pick, tokens, w, wt, out_w):
    vmem = pl.BlockSpec(memory_space=pltpu.VMEM)
    anywhere = pl.BlockSpec(memory_space=pl.ANY)
    columns = wt.shape[1]
    return pl.pallas_call(
        spatial_kernel,
        out_shape=[
            jax.ShapeDtypeStruct((BLOCK, D), BF16),
            jax.ShapeDtypeStruct((BLOCK, D), BF16),
            jax.ShapeDtypeStruct((HEADS, 2, 4, FRAGMENT, columns), BF16),
        ],
        in_specs=[pl.BlockSpec(memory_space=pltpu.SMEM), vmem, vmem, anywhere, vmem],
        out_specs=[vmem, vmem, anywhere],
        scratch_shapes=[
            pltpu.VMEM((4, 4, ROWS, D), BF16),
            pltpu.VMEM((4, 4, ROWS, D), BF16),
            pltpu.VMEM((4, 4, KEY_ROWS, D), BF16),
            pltpu.VMEM((8, KEY_ROWS, D), BF16),
            pltpu.VMEM((8, KEY_ROWS, D), BF16),
            pltpu.VMEM((4, KEY_ROWS, D), BF16),
            pltpu.VMEM((D, 3 * LANES), BF16),
            pltpu.VMEM((PATCHES, LANES), BF16),
            pltpu.VMEM((LANES, 2 * PATCHES), BF16),
            pltpu.VMEM((2 * PATCHES, LANES), BF16),
            pltpu.VMEM((16 * KEY_ROWS, 2 * LANES), BF16),
            pltpu.VMEM((8, 16 * KEY_ROWS, 2 * LANES), BF16),
            pltpu.VMEM((4, GROUP, LANES), F32),
            pltpu.VMEM((4, GROUP, LANES), F32),
            pltpu.VMEM((HEADS, HEAD_DIM, BLOCK), BF16),
            pltpu.VMEM((HEADS, HEAD_DIM, BLOCK), BF16),
            pltpu.SemaphoreType.DMA((COPIES,)),
            pltpu.SemaphoreType.DMA((COPIES,)),
            pltpu.SemaphoreType.DMA,
        ],
        compiler_params=pltpu.CompilerParams(
            collective_id=1, has_side_effects=True, vmem_limit_bytes=50 * 2**20
        ),
        name="spatial_branch",
    )(pick, tokens, w, wt, out_w)


HEAD_STEP = 4


def temporal_kernel(x_ref, wt_ref, o_ref, turned):
    step = pl.program_id(0)
    x = x_ref[...]
    row = lax.broadcasted_iota(jnp.int32, (BLOCK, BLOCK), 0)
    column = lax.broadcasted_iota(jnp.int32, (BLOCK, BLOCK), 1)
    same = (row & 3) == (column & 3)
    for h in range(HEAD_STEP):
        w = wt_ref[h].reshape(D, 3 * HEAD_DIM)
        qkv = jnp.dot(x, w, preferred_element_type=F32).astype(BF16)
        q, k = qkv[:, :HEAD_DIM], qkv[:, HEAD_DIM : 2 * HEAD_DIM]
        scores = lax.dot_general(
            q, k, (((1,), (1,)), ((), ())), preferred_element_type=F32
        ) * (HEAD_DIM**-0.5)
        scores = jnp.where(same, scores, -jnp.inf)
        exponent = jnp.exp(scores - jnp.max(scores, axis=-1, keepdims=True))
        weights = (exponent / jnp.sum(exponent, axis=-1, keepdims=True)).astype(BF16)
        out = jnp.dot(weights, qkv, preferred_element_type=F32)
        turned[step * HEAD_STEP + h] = out.T[2 * HEAD_DIM :, :]

    @pl.when(step == HEADS // HEAD_STEP - 1)
    def _():
        o_ref[...] = turned[...].reshape(D, BLOCK).T.astype(BF16)


def temporal_attend(x, wt):
    whole = pl.BlockSpec((BLOCK, D), lambda i: (0, 0))
    return pl.pallas_call(
        temporal_kernel,
        grid=(HEADS // HEAD_STEP,),
        out_shape=jax.ShapeDtypeStruct((BLOCK, D), BF16),
        in_specs=[
            whole,
            pl.BlockSpec((HEAD_STEP,) + wt.shape[1:], lambda i: (i, 0, 0, 0, 0)),
        ],
        out_specs=whole,
        scratch_shapes=[pltpu.VMEM((HEADS, HEAD_DIM, BLOCK), F32)],
        compiler_params=pltpu.CompilerParams(vmem_limit_bytes=48 * 2**20),
        name="temporal_attend",
    )(x, wt)


def per_device(tokens, key_frame, qkv_spatial, out_spatial, qkv_temporal):
    frame = lax.axis_index("frame")
    key = key_frame[0].astype(jnp.int32)
    y, zl, core = frame // 8, (frame // 2) % 4, frame % 2
    pick = jnp.stack(
        [(key // 8 - y) % 4 * 2 + (key % 2 - core) % 2, (key // 2 % 4 - zl) % 4]
    ).astype(jnp.int32)
    spatial, temporal_in, wt = spatial_branch(
        pick, tokens[0], qkv_spatial, qkv_temporal, out_spatial
    )
    rows = lax.all_to_all(
        temporal_in.reshape(32, 4, D), "frame", split_axis=0, concat_axis=0, tiled=True
    )
    mixed = temporal_attend(rows.reshape(BLOCK, D), wt)
    temporal = lax.all_to_all(
        mixed.reshape(32, 4, D), "frame", split_axis=0, concat_axis=0, tiled=True
    )
    return (spatial[None], temporal.reshape(1, BLOCK, D))


def solution(mesh):
    return jax.shard_map(
        per_device,
        mesh=mesh,
        in_specs=(P("frame", "patch", None), P(), P(None, "patch"), P(), P(None, "patch")),
        out_specs=(P("frame", "patch", None), P("frame", "patch", None)),
        check_vma=False,
    )
```

time: 254 us -> 206 us (0.81)
  Pallas kernels: 173 us -> 143 us
  blocking collectives: 66.7 us -> 39.7 us
  waiting for transfers between devices: 0 us -> 12 us
  local copies, waits for them, and re-layouts: 10.6 us -> 5.93 us
  starting transfers between devices: 0 us -> 3.66 us
    all_to_all x2 -> x0, blocking collectives: 42.7 us -> none  [the longest x1 27.3 us: per_device(): lax.all_to_all(heads, 'patch', split_axis=0, concat_axis=0, tiled=True)]
    pallas_call x3 -> x2, Pallas kernels: 173 us -> 143 us  [the longest x1 130 us: spatial_branch(): pl.pallas_call(spatial_kernel, out_shape=[jax.ShapeDtypeStruct((BLOCK, D)...]
    all_to_all x1, blocking collectives: 24 us -> 39.7 us  [per_device(): lax.all_to_all(temporal_in.reshape(32, 4, D), 'frame', split_axis=0, conc...]
    all_to_all x0 -> x1, waiting for transfers between devices: none -> 12 us  [per_device(): lax.all_to_all(mixed.reshape(32, 4, D), 'frame', split_axis=0, concat_axi...]
    all_to_all x0 -> x1, starting transfers between devices: none -> 3.66 us  [per_device(): lax.all_to_all(mixed.reshape(32, 4, D), 'frame', split_axis=0, concat_axi...]
    unnamed x11 -> x5, local copies, waits for them, and re-layouts: 5.82 us -> 4.21 us
  transfers between devices with their start and end apart: 0 -> 1, of which waited for: 0 -> 1; matrix products, arithmetic and copies ran while one was open for 0% -> 0% of each run, Pallas kernels for 0% -> 0%
where the time goes in v2:
time: 206 us
  Pallas kernels  143 us (69%)
  blocking collectives  39.7 us (19%)
  waiting for transfers between devices  12 us (6%)
  local copies, waits for them, and re-layouts  5.93 us (3%)
  starting transfers between devices  3.66 us (2%)
    pallas_call x1, Pallas kernels, spatial_branch(): pl.pallas_call(spatial_kernel, out_shape=[jax.ShapeDtypeStruct((BLOCK, D)...  130 us
    all_to_all x1, blocking collectives, per_device(): lax.all_to_all(temporal_in.reshape(32, 4, D), 'frame', split_axis=0, conc...  39.7 us
    pallas_call x1, Pallas kernels, temporal_attend(): pl.pallas_call(temporal_kernel, grid=(HEADS // HEAD_STEP,), out_shape=jax...  13.5 us
    all_to_all x1, waiting for transfers between devices, per_device(): lax.all_to_all(mixed.reshape(32, 4, D), 'frame', split_axis=0, concat_axi...  12 us
    unnamed x5, local copies, waits for them, and re-layouts  4.21 us
  transfers between devices with their start and end apart: 1, of which 1 were waited for; matrix products, arithmetic and copies ran while one was open for 0% of the time, Pallas kernels for 0%

profile of v2, /device:TPU:1, one launch (start us, length us, event | category | flops | bytes accessed | tf_op | source)
XLA Modules:
  0.0 206.1 jit_solution(3545348671900975751)
XLA Ops:
  1.4 1.3 copy.7.w_ref
  2.7 1.3 copy.8.wt_ref
  4.0 0.1 pad_add_fusion.pick_ref
  4.1 0.0 copy-start
  4.1 1.0 copy-done
  5.0 129.8 %spatial_branch.1 = (bf16[128,1152]{1,0:T(8,128)(2,1)S(1)}, bf16[128,1152]{1,0:T(8,128)(2,1)S(1)}, bf16[16,2,4,144,216]{4,3,2,1,0:T(8,128)(2,1)}) custom-call(s32[2]{0:T(128)S(1)} %pad_add_fusion.pick_ref, bf16[128,1152]{1,0:T(8,128)(2,1)S(1)} %bitcast.9, bf16[1152,216]{1,0:T(8,128)(2,1)S(1)} %copy.7.w_ref, bf16[1152,216]{1,0:T(8,128)(2,1)S(1)} %copy.8.wt_ref, ...), custom_call_target="tpu_custom_call" | custom-call | tf_op jit(solution)/shard_map/spatial_branch/pallas_call | solution.py:386
  134.8 0.1 reshape.16
  134.9 39.7 %all_to_all.10 = bf16[32,4,1152]{2,1,0:T(4,128)(2,1)S(1)} all-to-all(bf16[32,4,1152]{2,1,0:T(4,128)(2,1)S(1)} %reshape.16), channel_id=1, replica_groups=mesh['frame'=32,'patch'=16] {'frame'}, dimensions={0} | all-to-all | bytes 589824 | tf_op jit(solution)/shard_map/all_to_all | solution.py:477
  174.5 0.1 reshape.17.x_ref
  174.6 13.5 %temporal_attend.1 = bf16[128,1152]{1,0:T(8,128)(2,1)S(1)} custom-call(bf16[128,1152]{1,0:T(8,128)(2,1)S(1)} %reshape.17.x_ref, bf16[16,2,4,144,216]{4,3,2,1,0:T(8,128)(2,1)} %get-tuple-element.7.wt_ref), custom_call_target="tpu_custom_call" | custom-call | tf_op jit(solution)/shard_map/temporal_attend/pallas_call | solution.py:452
  188.1 0.8 reshape.18
  188.9 3.7 %all-to-all-start.1 = ((bf16[32,4,1152]{2,1,0:T(4,128)(2,1)}), bf16[32,4,1152]{2,1,0:T(4,128)(2,1)S(1)}, u32[]{:S(2)}, u32[]{:S(2)}) async-start(bf16[32,4,1152]{2,1,0:T(4,128)(2,1)} %reshape.18), calls=%async_computation.1 | async-start | bytes 589824 | tf_op jit(solution)/shard_map/all_to_all | solution.py:481
  192.6 12.0 %all-to-all-done.1 = bf16[32,4,1152]{2,1,0:T(4,128)(2,1)S(1)} async-done(((bf16[32,4,1152]{2,1,0:T(4,128)(2,1)}), bf16[32,4,1152]{2,1,0:T(4,128)(2,1)S(1)}, u32[]{:S(2)}, u32[]{:S(2)}) %all-to-all-start.1) | async-done | bytes 294944 | tf_op jit(solution)/shard_map/all_to_all | solution.py:481
  204.6 0.8 reshape.19
  205.4 0.7 copy.11
Async XLA Ops:
  4.1 1.0 copy-start
  188.9 15.7 %all-to-all-start.1 = ((bf16[32,4,1152]{2,1,0:T(4,128)(2,1)}), bf16[32,4,1152]{2,1,0:T(4,128)(2,1)S(1)}, u32[]{:S(2)}, u32[]{:S(2)}) async-start(bf16[32,4,1152]{2,1,0:T(4,128)(2,1)} %reshape.18), calls=%async_computation.1 | async-start | bytes 589824 | tf_op jit(solution)/shard_map/all_to_all | solution.py:481

commit v3 on v2

--- a/solution.py
+++ b/solution.py
@@ -215,6 +215,7 @@
     for c in range(CHUNKS):
         held[c][0, 0] = normed[c * ROWS : (c + 1) * ROWS]
     gathers = [Gather(links, held[c], ROWS) for c in range(CHUNKS)]
+    gathers[0].begin_z()
     for one in gathers:
         one.send_x(0)
     mine = wt_ref.at[pl.ds(pl.multiple_of((core * 4 + y) * FRAGMENT, 16), FRAGMENT)]
@@ -229,26 +230,23 @@
         links.copy(second.at[0], second.at[4 - dz], links.frame_device(0, dz, 0))
         for dz in (1, 2, 3)
     ]
-    for one in gathers:
-        one.begin_z()
-    wt_up = links.copy(mine, place, links.patch_device(0, 1))
-    wt_down = links.copy(mine, place, links.patch_device(0, 3))
+    gathers[1].begin_z()
     w[...] = jnp.zeros_like(w)
     for i in range(3):
         w[:, i * LANES : i * LANES + HEAD_DIM] = w_ref[:, i * HEAD_DIM : (i + 1) * HEAD_DIM]
+    for one in gathers:
+        one.forward_x(0)
+    gathers[0].neighbours()
     for made in picks:
         made.wait_recv()
     kheld[0, 0] = second[pick_ref[1]]
     keys = Gather(links, kheld, KEY_ROWS)
+    keys.begin_z()
     keys.send_x(0)
-    keys.begin_z()
-    for one in gathers:
-        one.forward_x(0)
-    for one in (gathers[0], gathers[1], keys):
-        one.neighbours()
-    wt_up.wait_recv()
-    below = wt.at[x * 4 + turn(links.zh, 3), core, y]
-    wt_far = links.copy(below, below, links.patch_device(0, 1))
+    gathers[1].neighbours()
+    wt_up = links.copy(mine, place, links.patch_device(0, 1))
+    wt_down = links.copy(mine, place, links.patch_device(0, 3))
+    keys.neighbours()
     keys.forward_x(0)
 
     def finish(dz):
@@ -267,33 +265,41 @@
 
     finish(0)
     for dz in (3, 1):
-        for one in (gathers[0], gathers[1], keys):
+        for one in (gathers[0], gathers[1]):
             one.forward_x(dz)
+    for one in (gathers[0], gathers[1]):
+        one.opposite()
+    for dz in (3, 1):
+        keys.forward_x(dz)
+    keys.opposite()
+    wt_up.wait_recv()
+    below = wt.at[x * 4 + turn(links.zh, 3), core, y]
+    wt_far = links.copy(below, below, links.patch_device(0, 1))
+    finish(3)
+    finish(1)
     for one in (gathers[0], gathers[1], keys):
-        one.opposite()
+        one.forward_x(2)
     own.wait()
     wt_down.wait_recv()
     wt_far.wait_recv()
     group = pl.ds(x * 4, 4)
     upper, lower = pl.ds(0, SPLIT), pl.ds(SPLIT, FRAGMENT - SPLIT)
     by_y, by_x = wt.at[group, core, y, upper], wt.at[group, core, y, lower]
-    steps = []
-    for d in (1, 3, 2):
-        steps.append(links.copy(by_y, by_y, links.frame_device(d, 0, 0)))
-        steps.append(links.copy(by_x, by_x, links.patch_device(d, 0)))
-    finish(3)
-    finish(1)
-    for one in (gathers[0], gathers[1], keys):
-        one.forward_x(2)
     for dz in range(4):
         keys.done_x(dz)
     kv_out[...] = jnp.dot(
         kheld[...].reshape(16 * KEY_ROWS, D), w[:, LANES:], preferred_element_type=F32
     ).astype(BF16)
-    kv = [
-        links.copy(kv_out, kv_in.at[(4 - dy) % 4 * 2 + dc], links.frame_device(dy, 0, dc))
-        for dy, dc in others
+    twin = links.frame_device(0, 0, 1)
+    kv_y = [
+        (links.copy(kv_out, kv_in.at[(4 - d) * 2], links.frame_device(d, 0, 0)), (4 - d) * 2)
+        for d in (1, 3, 2)
     ]
+    kv_twin = [links.copy(kv_out, kv_in.at[1], twin)]
+    steps = []
+    for d in (1, 3, 2):
+        steps.append(links.copy(by_y, by_y, links.frame_device(d, 0, 0)))
+        steps.append(links.copy(by_x, by_x, links.patch_device(d, 0)))
     finish(2)
     for made in steps:
         made.wait_recv()
@@ -306,7 +312,6 @@
     def pass_on(piece, device):
         return links.copy(piece, piece, device)
 
-    twin = links.frame_device(0, 0, 1)
     x_up = pass_on(along_x(0), links.patch_device(1, 0))
     x_down = pass_on(along_x(0), links.patch_device(3, 0))
     y_up = pass_on(along_y(0), links.frame_device(1, 0, 0))
@@ -323,8 +328,12 @@
         weights = jnp.exp2(scores - largest).astype(BF16)
         total_s[g] = jnp.dot(weights, v_s[:PATCHES, :], preferred_element_type=F32)
         largest_s[g] = jnp.broadcast_to(largest, (GROUP, LANES))
+        if g == 0:
+            for made, slot in kv_y:
+                made.wait_recv()
+                kv_twin.append(links.copy(kv_in.at[slot], kv_in.at[slot + 1], twin))
     kv_in[0] = kv_out[...]
-    for made in kv:
+    for made in kv_twin:
         made.wait_recv()
     for g in range(8):
         at = PATCHES + g * 16 * KEY_ROWS

time: 206 us -> 192 us (0.932)
  blocking collectives: 39.7 us -> 23.4 us
    all_to_all x1, blocking collectives: 39.7 us -> 23.4 us  [per_device(): lax.all_to_all(temporal_in.reshape(32, 4, D), 'frame', split_axis=0, conc...]
where the time goes in v3:
time: 192 us
  Pallas kernels  145 us (76%)
  blocking collectives  23.4 us (12%)
  waiting for transfers between devices  12 us (6%)
  local copies, waits for them, and re-layouts  5.93 us (3%)
  starting transfers between devices  3.66 us (2%)
    pallas_call x1, Pallas kernels, spatial_branch(): pl.pallas_call(spatial_kernel, out_shape=[jax.ShapeDtypeStruct((BLOCK, D)...  131 us
    all_to_all x1, blocking collectives, per_device(): lax.all_to_all(temporal_in.reshape(32, 4, D), 'frame', split_axis=0, conc...  23.4 us
    pallas_call x1, Pallas kernels, temporal_attend(): pl.pallas_call(temporal_kernel, grid=(HEADS // HEAD_STEP,), out_shape=jax...  13.5 us
    all_to_all x1, waiting for transfers between devices, per_device(): lax.all_to_all(mixed.reshape(32, 4, D), 'frame', split_axis=0, concat_axi...  12 us
    unnamed x5, local copies, waits for them, and re-layouts  4.21 us
  transfers between devices with their start and end apart: 1, of which 1 were waited for; matrix products, arithmetic and copies ran while one was open for 0% of the time, Pallas kernels for 0%

profile of v3, /device:TPU:1, one launch (start us, length us, event | category | flops | bytes accessed | tf_op | source)
XLA Modules:
  0.0 191.5 jit_solution(15315611179393871223)
XLA Ops:
  1.4 1.3 copy.7.w_ref
  2.7 1.3 copy.8.wt_ref
  4.0 0.1 pad_add_fusion.pick_ref
  4.1 0.0 copy-start
  4.1 1.0 copy-done
  5.0 131.5 %spatial_branch.1 = (bf16[128,1152]{1,0:T(8,128)(2,1)S(1)}, bf16[128,1152]{1,0:T(8,128)(2,1)S(1)}, bf16[16,2,4,144,216]{4,3,2,1,0:T(8,128)(2,1)}) custom-call(s32[2]{0:T(128)S(1)} %pad_add_fusion.pick_ref, bf16[128,1152]{1,0:T(8,128)(2,1)S(1)} %bitcast.9, bf16[1152,216]{1,0:T(8,128)(2,1)S(1)} %copy.7.w_ref, bf16[1152,216]{1,0:T(8,128)(2,1)S(1)} %copy.8.wt_ref, ...), custom_call_target="tpu_custom_call" | custom-call | tf_op jit(solution)/shard_map/spatial_branch/pallas_call | solution.py:395
  136.5 0.1 reshape.16
  136.6 23.4 %all_to_all.10 = bf16[32,4,1152]{2,1,0:T(4,128)(2,1)S(1)} all-to-all(bf16[32,4,1152]{2,1,0:T(4,128)(2,1)S(1)} %reshape.16), channel_id=1, replica_groups=mesh['frame'=32,'patch'=16] {'frame'}, dimensions={0} | all-to-all | bytes 589824 | tf_op jit(solution)/shard_map/all_to_all | solution.py:486
  160.0 0.1 reshape.17.x_ref
  160.0 13.5 %temporal_attend.1 = bf16[128,1152]{1,0:T(8,128)(2,1)S(1)} custom-call(bf16[128,1152]{1,0:T(8,128)(2,1)S(1)} %reshape.17.x_ref, bf16[16,2,4,144,216]{4,3,2,1,0:T(8,128)(2,1)} %get-tuple-element.7.wt_ref), custom_call_target="tpu_custom_call" | custom-call | tf_op jit(solution)/shard_map/temporal_attend/pallas_call | solution.py:461
  173.5 0.8 reshape.18
  174.3 3.7 %all-to-all-start.1 = ((bf16[32,4,1152]{2,1,0:T(4,128)(2,1)}), bf16[32,4,1152]{2,1,0:T(4,128)(2,1)S(1)}, u32[]{:S(2)}, u32[]{:S(2)}) async-start(bf16[32,4,1152]{2,1,0:T(4,128)(2,1)} %reshape.18), calls=%async_computation.1 | async-start | bytes 589824 | tf_op jit(solution)/shard_map/all_to_all | solution.py:490
  178.0 12.0 %all-to-all-done.1 = bf16[32,4,1152]{2,1,0:T(4,128)(2,1)S(1)} async-done(((bf16[32,4,1152]{2,1,0:T(4,128)(2,1)}), bf16[32,4,1152]{2,1,0:T(4,128)(2,1)S(1)}, u32[]{:S(2)}, u32[]{:S(2)}) %all-to-all-start.1) | async-done | bytes 294944 | tf_op jit(solution)/shard_map/all_to_all | solution.py:490
  190.0 0.8 reshape.19
  190.8 0.7 copy.11
Async XLA Ops:
  4.1 1.0 copy-start
  174.3 15.7 %all-to-all-start.1 = ((bf16[32,4,1152]{2,1,0:T(4,128)(2,1)}), bf16[32,4,1152]{2,1,0:T(4,128)(2,1)S(1)}, u32[]{:S(2)}, u32[]{:S(2)}) async-start(bf16[32,4,1152]{2,1,0:T(4,128)(2,1)} %reshape.18), calls=%async_computation.1 | async-start | bytes 589824 | tf_op jit(solution)/shard_map/all_to_all | solution.py:490

commit v4 on v3

--- a/solution.py
+++ b/solution.py
@@ -11,7 +11,9 @@
 HEADS = 16
 HEAD_DIM = 72
 PATCHES = 2048
+FRAMES = 32
 BLOCK = 128
+GROUP_ROWS = BLOCK // FRAMES
 LANES = 128
 CHUNKS = 2
 ROWS = BLOCK // CHUNKS
@@ -56,6 +58,9 @@
     def frame_device(self, dy, dz, dc):
         frame = turn(self.y, dy) * 8 + turn(self.zl, dz) * 2 + lax.rem(self.core + dc, 2)
         return (frame, self.patch)
+
+    def frame_at(self, by):
+        return (lax.rem(self.frame + by, FRAMES), self.patch)
 
     def copy(self, src, dst, device):
         made = pltpu.make_async_remote_copy(
@@ -158,19 +163,74 @@
 
 
 GATHER_COPIES = 20
-COPIES = (CHUNKS + 1) * GATHER_COPIES + 7 + 3 + 7 + 3 + 6 + 6 + 8 + 15
-SPLIT = 80
+COPIES = (CHUNKS + 1) * GATHER_COPIES + 7 + 3 + 7 + 3 + 6 + 6 + 8 + 15 + 62
+SPLIT = 64
 GROUP = 512
 
 
-def spatial_kernel(
+HEAD_STEP = 4
+
+
+def scatter(links, values, out, landing):
+    for f in range(FRAMES):
+        out[f] = values[f * GROUP_ROWS : (f + 1) * GROUP_ROWS].astype(BF16)
+    links.slots = [
+        links.copy(
+            out.at[lax.rem(links.frame + k, FRAMES)], landing.at[links.frame], links.frame_at(k)
+        )
+        for k in range(1, FRAMES)
+    ]
+    landing[links.frame] = out[links.frame]
+
+
+def collect(links, landing, flat):
+    for made in links.slots:
+        made.wait_recv()
+    for f in range(FRAMES):
+        flat[f * GROUP_ROWS : (f + 1) * GROUP_ROWS, :] = landing[f].astype(F32)
+
+
+def mix(rows, wt, turned, first):
+    row = lax.broadcasted_iota(jnp.int32, (BLOCK, BLOCK), 0)
+    column = lax.broadcasted_iota(jnp.int32, (BLOCK, BLOCK), 1)
+    same = lax.rem(row, GROUP_ROWS) == lax.rem(column, GROUP_ROWS)
+    heads = range(first, first + HEAD_STEP)
+    qkv = [
+        jnp.dot(
+            rows, wt[h].reshape(D, 3 * HEAD_DIM), preferred_element_type=F32
+        ).astype(BF16)
+        for h in heads
+    ]
+    scores = [
+        lax.dot_general(
+            one[:, :HEAD_DIM],
+            one[:, HEAD_DIM : 2 * HEAD_DIM],
+            (((1,), (1,)), ((), ())),
+            preferred_element_type=F32,
+        )
+        * (HEAD_DIM**-0.5)
+        for one in qkv
+    ]
+    scores = [jnp.where(same, one, -jnp.inf) for one in scores]
+    largest = [jnp.max(one, axis=-1, keepdims=True) for one in scores]
+    exponent = [jnp.exp(one - top) for one, top in zip(scores, largest)]
+    sums = [jnp.sum(one, axis=-1, keepdims=True) for one in exponent]
+    weights = [(one / total).astype(BF16) for one, total in zip(exponent, sums)]
+    outs = [
+        jnp.dot(one, values, preferred_element_type=F32) for one, values in zip(weights, qkv)
+    ]
+    for h, out in zip(heads, outs):
+        turned[h] = out.T[2 * HEAD_DIM :, :]
+
+
+def block_kernel(
     pick_ref,
     tokens_ref,
     w_ref,
     wt_ref,
     out_w_ref,
     spatial_ref,
-    normed_ref,
+    temporal_ref,
     wt,
     held0,
     held1,
@@ -188,6 +248,12 @@
     largest_s,
     out_s,
     heads,
+    rows_out,
+    rows_in,
+    mixed_out,
+    mixed_in,
+    flat,
+    head_rows,
     send,
     recv,
     local_sem,
@@ -198,8 +264,7 @@
     turns = [(dz, dx) for dz in (0, 3, 1, 2) for dx in range(4)]
     greet(
         [links.patch_device(dx, dz) for dz, dx in turns if (dz, dx) != (0, 0)]
-        + [links.frame_device(dy, 0, dc) for dy, dc in others]
-        + [links.frame_device(0, dz, 0) for dz in (1, 2, 3)]
+        + [links.frame_at(k) for k in range(1, FRAMES)]
     )
     held = (held0, held1)
     normed = rms_norm(tokens_ref[...]).astype(BF16)
@@ -340,7 +405,7 @@
         kt[:, at : at + 16 * KEY_ROWS] = kv_in[g, :, :LANES].T
         v_s[at : at + 16 * KEY_ROWS, :] = with_ones(kv_in[g, :, LANES:].astype(F32)).astype(BF16)
     sent = []
-    for i, g in enumerate((2, 3, 1, 0)):
+    for g in (2, 3, 1, 0):
         scores, new = scores_of(g, slice(PATCHES, 2 * PATCHES))
         largest = largest_s[g][:, :1]
         new = jnp.maximum(largest, new)
@@ -360,48 +425,54 @@
                         out_s.at[g * 4 + dx], heads.at[links.patch], links.patch_device(dx, g)
                     )
                 )
-        if i == 1:
-            x_up.wait_recv()
-            far = [pass_on(along_x(3, half=slice(0, 2)), links.patch_device(1, 0))]
-            cross.append(pass_on(along_x(3), twin))
-            y_up.wait_recv()
-            far.append(pass_on(along_y(3, slice(0, 8)), links.frame_device(1, 0, 0)))
-            cross.append(pass_on(along_y(3), twin))
-            x_down.wait_recv()
-            far.append(pass_on(along_x(1, half=slice(2, 4)), links.patch_device(3, 0)))
-            cross.append(pass_on(along_x(1), twin))
-            y_down.wait_recv()
-            far.append(pass_on(along_y(1, slice(8, 16)), links.frame_device(3, 0, 0)))
-            cross.append(pass_on(along_y(1), twin))
+    x_up.wait_recv()
+    far = [pass_on(along_x(3, half=slice(0, 2)), links.patch_device(1, 0))]
+    cross.append(pass_on(along_x(3), twin))
+    y_up.wait_recv()
+    far.append(pass_on(along_y(3, slice(0, 8)), links.frame_device(1, 0, 0)))
+    cross.append(pass_on(along_y(3), twin))
+    x_down.wait_recv()
+    far.append(pass_on(along_x(1, half=slice(2, 4)), links.patch_device(3, 0)))
+    cross.append(pass_on(along_x(1), twin))
+    y_down.wait_recv()
+    far.append(pass_on(along_y(1, slice(8, 16)), links.frame_device(3, 0, 0)))
+    cross.append(pass_on(along_y(1), twin))
     for made in sent:
         made.wait_recv()
     rows = heads[...].reshape(D, BLOCK).T
     spatial = jnp.dot(rows, out_w_ref[...], preferred_element_type=F32).astype(BF16)
     spatial_ref[...] = spatial
-    normed_ref[...] = rms_norm(spatial).astype(BF16)
+    scatter(links, rms_norm(spatial), rows_out, rows_in)
     for made in far:
         made.wait_recv()
     cross.append(pass_on(along_x(2), twin))
     cross.append(pass_on(along_y(2), twin))
+    collect(links, rows_in, flat)
+    rows = flat[...].astype(BF16)
     for made in cross:
         made.wait_recv()
+    for h in range(0, HEADS, HEAD_STEP):
+        mix(rows, wt, head_rows, h)
+    scatter(links, head_rows[...].reshape(D, BLOCK).T, mixed_out, mixed_in)
+    collect(links, mixed_in, flat)
+    temporal_ref[...] = flat[...].astype(BF16)
     links.finish()
 
 
-def spatial_branch(pick, tokens, w, wt, out_w):
+def block(pick, tokens, w, wt, out_w):
     vmem = pl.BlockSpec(memory_space=pltpu.VMEM)
     anywhere = pl.BlockSpec(memory_space=pl.ANY)
     columns = wt.shape[1]
     return pl.pallas_call(
-        spatial_kernel,
+        block_kernel,
         out_shape=[
             jax.ShapeDtypeStruct((BLOCK, D), BF16),
             jax.ShapeDtypeStruct((BLOCK, D), BF16),
-            jax.ShapeDtypeStruct((HEADS, 2, 4, FRAGMENT, columns), BF16),
         ],
         in_specs=[pl.BlockSpec(memory_space=pltpu.SMEM), vmem, vmem, anywhere, vmem],
-        out_specs=[vmem, vmem, anywhere],
+        out_specs=[vmem, vmem],
         scratch_shapes=[
+            pltpu.VMEM((HEADS, 2, 4, FRAGMENT, columns), BF16),
             pltpu.VMEM((4, 4, ROWS, D), BF16),
             pltpu.VMEM((4, 4, ROWS, D), BF16),
             pltpu.VMEM((4, 4, KEY_ROWS, D), BF16),
@@ -418,6 +489,12 @@
             pltpu.VMEM((4, GROUP, LANES), F32),
             pltpu.VMEM((HEADS, HEAD_DIM, BLOCK), BF16),
             pltpu.VMEM((HEADS, HEAD_DIM, BLOCK), BF16),
+            pltpu.VMEM((FRAMES, GROUP_ROWS, D), BF16),
+            pltpu.VMEM((FRAMES, GROUP_ROWS, D), BF16),
+            pltpu.VMEM((FRAMES, GROUP_ROWS, D), BF16),
+            pltpu.VMEM((FRAMES, GROUP_ROWS, D), BF16),
+            pltpu.VMEM((BLOCK, D), F32),
+            pltpu.VMEM((HEADS, HEAD_DIM, BLOCK), F32),
             pltpu.SemaphoreType.DMA((COPIES,)),
             pltpu.SemaphoreType.DMA((COPIES,)),
             pltpu.SemaphoreType.DMA,
@@ -425,52 +502,8 @@
         compiler_params=pltpu.CompilerParams(
             collective_id=1, has_side_effects=True, vmem_limit_bytes=50 * 2**20
         ),
-        name="spatial_branch",
+        name="block",
     )(pick, tokens, w, wt, out_w)
-
-
-HEAD_STEP = 4
-
-
-def temporal_kernel(x_ref, wt_ref, o_ref, turned):
-    step = pl.program_id(0)
-    x = x_ref[...]
-    row = lax.broadcasted_iota(jnp.int32, (BLOCK, BLOCK), 0)
-    column = lax.broadcasted_iota(jnp.int32, (BLOCK, BLOCK), 1)
-    same = (row & 3) == (column & 3)
-    for h in range(HEAD_STEP):
-        w = wt_ref[h].reshape(D, 3 * HEAD_DIM)
-        qkv = jnp.dot(x, w, preferred_element_type=F32).astype(BF16)
-        q, k = qkv[:, :HEAD_DIM], qkv[:, HEAD_DIM : 2 * HEAD_DIM]
-        scores = lax.dot_general(
-            q, k, (((1,), (1,)), ((), ())), preferred_element_type=F32
-        ) * (HEAD_DIM**-0.5)
-        scores = jnp.where(same, scores, -jnp.inf)
-        exponent = jnp.exp(scores - jnp.max(scores, axis=-1, keepdims=True))
-        weights = (exponent / jnp.sum(exponent, axis=-1, keepdims=True)).astype(BF16)
-        out = jnp.dot(weights, qkv, preferred_element_type=F32)
-        turned[step * HEAD_STEP + h] = out.T[2 * HEAD_DIM :, :]
-
-    @pl.when(step == HEADS // HEAD_STEP - 1)
-    def _():
-        o_ref[...] = turned[...].reshape(D, BLOCK).T.astype(BF16)
-
-
-def temporal_attend(x, wt):
-    whole = pl.BlockSpec((BLOCK, D), lambda i: (0, 0))
-    return pl.pallas_call(
-        temporal_kernel,
-        grid=(HEADS // HEAD_STEP,),
-        out_shape=jax.ShapeDtypeStruct((BLOCK, D), BF16),
-        in_specs=[
-            whole,
-            pl.BlockSpec((HEAD_STEP,) + wt.shape[1:], lambda i: (i, 0, 0, 0, 0)),
-        ],
-        out_specs=whole,
-        scratch_shapes=[pltpu.VMEM((HEADS, HEAD_DIM, BLOCK), F32)],
-        compiler_params=pltpu.CompilerParams(vmem_limit_bytes=48 * 2**20),
-        name="temporal_attend",
-    )(x, wt)
 
 
 def per_device(tokens, key_frame, qkv_spatial, out_spatial, qkv_temporal):
@@ -480,17 +513,10 @@
     pick = jnp.stack(
         [(key // 8 - y) % 4 * 2 + (key % 2 - core) % 2, (key // 2 % 4 - zl) % 4]
     ).astype(jnp.int32)
-    spatial, temporal_in, wt = spatial_branch(
+    spatial, temporal = block(
         pick, tokens[0], qkv_spatial, qkv_temporal, out_spatial
     )
-    rows = lax.all_to_all(
-        temporal_in.reshape(32, 4, D), "frame", split_axis=0, concat_axis=0, tiled=True
-    )
-    mixed = temporal_attend(rows.reshape(BLOCK, D), wt)
-    temporal = lax.all_to_all(
-        mixed.reshape(32, 4, D), "frame", split_axis=0, concat_axis=0, tiled=True
-    )
-    return (spatial[None], temporal.reshape(1, BLOCK, D))
+    return (spatial[None], temporal[None])
 
 
 def solution(mesh):

time: 192 us -> 160 us (0.83)
  blocking collectives: 23.4 us -> 0 us
  waiting for transfers between devices: 12 us -> 0 us
  Pallas kernels: 145 us -> 153 us
  starting transfers between devices: 3.66 us -> 0 us
    all_to_all x1 -> x0, blocking collectives: 23.4 us -> none  [per_device(): lax.all_to_all(temporal_in.reshape(32, 4, D), 'frame', split_axis=0, conc...]
    all_to_all x1 -> x0, waiting for transfers between devices: 12 us -> none  [per_device(): lax.all_to_all(mixed.reshape(32, 4, D), 'frame', split_axis=0, concat_axi...]
    pallas_call x2 -> x1, Pallas kernels: 145 us -> 153 us  [block(): pl.pallas_call(block_kernel, out_shape=[jax.ShapeDtypeStruct((BLOCK, D),...]
    all_to_all x1 -> x0, starting transfers between devices: 3.66 us -> none  [per_device(): lax.all_to_all(mixed.reshape(32, 4, D), 'frame', split_axis=0, concat_axi...]
    unnamed x5 -> x6, local copies, waits for them, and re-layouts: 4.21 us -> 4.92 us
  transfers between devices with their start and end apart: 1 -> 0, of which waited for: 1 -> 0; matrix products, arithmetic and copies ran while one was open for 0% -> 0% of each run, Pallas kernels for 0% -> 0%
where the time goes in v4:
time: 160 us
  Pallas kernels  153 us (96%)
  local copies, waits for them, and re-layouts  4.92 us (3%)
    pallas_call x1, Pallas kernels, block(): pl.pallas_call(block_kernel, out_shape=[jax.ShapeDtypeStruct((BLOCK, D),...  153 us
    unnamed x6, local copies, waits for them, and re-layouts  4.92 us

profile of v4, /device:TPU:1, one launch (start us, length us, event | category | flops | bytes accessed | tf_op | source)
XLA Modules:
  0.0 159.8 jit_solution(11634924924920246796)
XLA Ops:
  1.4 0.1 pad_add_fusion.pick_ref
  1.5 1.3 copy.7.w_ref
  2.8 1.3 copy.8.wt_ref
  4.0 0.0 copy-start
  4.1 1.0 copy-done
  5.0 153.3 %block.1 = (bf16[128,1152]{1,0:T(8,128)(2,1)S(1)}, bf16[128,1152]{1,0:T(8,128)(2,1)S(1)}) custom-call(s32[2]{0:T(128)S(1)} %pad_add_fusion.pick_ref, bf16[128,1152]{1,0:T(8,128)(2,1)S(1)} %bitcast.10, bf16[1152,216]{1,0:T(8,128)(2,1)S(1)} %copy.7.w_ref, bf16[1152,216]{1,0:T(8,128)(2,1)S(1)} %copy.8.wt_ref, bf16[1152,1152]{1,0:T(8,128)(2,1)} %out_w_ref.1), custom_call_target="tpu_custom_call" | custom-call | tf_op jit(solution)/shard_map/block/pallas_call | solution.py:466
  158.3 0.7 copy.12
  159.1 0.7 copy.13
Async XLA Ops:
  4.0 1.0 copy-start

commit v5 on v4

--- a/solution.py
+++ b/solution.py
@@ -337,19 +337,13 @@
     for dz in (3, 1):
         keys.forward_x(dz)
     keys.opposite()
-    wt_up.wait_recv()
-    below = wt.at[x * 4 + turn(links.zh, 3), core, y]
-    wt_far = links.copy(below, below, links.patch_device(0, 1))
     finish(3)
     finish(1)
     for one in (gathers[0], gathers[1], keys):
         one.forward_x(2)
-    own.wait()
-    wt_down.wait_recv()
-    wt_far.wait_recv()
-    group = pl.ds(x * 4, 4)
-    upper, lower = pl.ds(0, SPLIT), pl.ds(SPLIT, FRAGMENT - SPLIT)
-    by_y, by_x = wt.at[group, core, y, upper], wt.at[group, core, y, lower]
+    wt_up.wait_recv()
+    below = wt.at[x * 4 + turn(links.zh, 3), core, y]
+    wt_far = links.copy(below, below, links.patch_device(0, 1))
     for dz in range(4):
         keys.done_x(dz)
     kv_out[...] = jnp.dot(
@@ -361,13 +355,18 @@
         for d in (1, 3, 2)
     ]
     kv_twin = [links.copy(kv_out, kv_in.at[1], twin)]
+    finish(2)
+    own.wait()
+    wt_down.wait_recv()
+    wt_far.wait_recv()
+    group = pl.ds(x * 4, 4)
+    upper, lower = pl.ds(0, SPLIT), pl.ds(SPLIT, FRAGMENT - SPLIT)
+    by_y, by_x = wt.at[group, core, y, upper], wt.at[group, core, y, lower]
     steps = []
     for d in (1, 3, 2):
         steps.append(links.copy(by_y, by_y, links.frame_device(d, 0, 0)))
         steps.append(links.copy(by_x, by_x, links.patch_device(d, 0)))
-    finish(2)
-    for made in steps:
-        made.wait_recv()
+
     def along_x(dx, rows=upper, half=slice(0, 4)):
         return wt.at[pl.ds(turn(x, dx) * 4, 4), core, pl.ds(half.start, half.stop - half.start), rows]
 
@@ -376,12 +375,6 @@
 
     def pass_on(piece, device):
         return links.copy(piece, piece, device)
-
-    x_up = pass_on(along_x(0), links.patch_device(1, 0))
-    x_down = pass_on(along_x(0), links.patch_device(3, 0))
-    y_up = pass_on(along_y(0), links.frame_device(1, 0, 0))
-    y_down = pass_on(along_y(0), links.frame_device(3, 0, 0))
-    cross = [pass_on(along_x(0), twin), pass_on(along_y(0), twin)]
 
     def scores_of(g, keys):
         q = q_s[g * GROUP : (g + 1) * GROUP, :]
@@ -397,6 +390,13 @@
             for made, slot in kv_y:
                 made.wait_recv()
                 kv_twin.append(links.copy(kv_in.at[slot], kv_in.at[slot + 1], twin))
+    for made in steps:
+        made.wait_recv()
+    x_up = pass_on(along_x(0), links.patch_device(1, 0))
+    x_down = pass_on(along_x(0), links.patch_device(3, 0))
+    y_up = pass_on(along_y(0), links.frame_device(1, 0, 0))
+    y_down = pass_on(along_y(0), links.frame_device(3, 0, 0))
+    cross = [pass_on(along_x(0), twin), pass_on(along_y(0), twin)]
     kv_in[0] = kv_out[...]
     for made in kv_twin:
         made.wait_recv()
@@ -425,6 +425,12 @@
                         out_s.at[g * 4 + dx], heads.at[links.patch], links.patch_device(dx, g)
                     )
                 )
+    for made in sent:
+        made.wait_recv()
+    rows = heads[...].reshape(D, BLOCK).T
+    spatial = jnp.dot(rows, out_w_ref[...], preferred_element_type=F32).astype(BF16)
+    spatial_ref[...] = spatial
+    scatter(links, rms_norm(spatial), rows_out, rows_in)
     x_up.wait_recv()
     far = [pass_on(along_x(3, half=slice(0, 2)), links.patch_device(1, 0))]
     cross.append(pass_on(along_x(3), twin))
@@ -437,12 +443,6 @@
     y_down.wait_recv()
     far.append(pass_on(along_y(1, slice(8, 16)), links.frame_device(3, 0, 0)))
     cross.append(pass_on(along_y(1), twin))
-    for made in sent:
-        made.wait_recv()
-    rows = heads[...].reshape(D, BLOCK).T
-    spatial = jnp.dot(rows, out_w_ref[...], preferred_element_type=F32).astype(BF16)
-    spatial_ref[...] = spatial
-    scatter(links, rms_norm(spatial), rows_out, rows_in)
     for made in far:
         made.wait_recv()
     cross.append(pass_on(along_x(2), twin))

time: 160 us -> 155 us (0.969)
  Pallas kernels: 153 us -> 148 us
    pallas_call x1, Pallas kernels: 153 us -> 148 us  [block(): pl.pallas_call(block_kernel, out_shape=[jax.ShapeDtypeStruct((BLOCK, D),...]
where the time goes in v5:
time: 155 us
  Pallas kernels  148 us (95%)
  local copies, waits for them, and re-layouts  4.92 us (3%)
    pallas_call x1, Pallas kernels, block(): pl.pallas_call(block_kernel, out_shape=[jax.ShapeDtypeStruct((BLOCK, D),...  148 us
    unnamed x6, local copies, waits for them, and re-layouts  4.92 us

profile of v5, /device:TPU:1, one launch (start us, length us, event | category | flops | bytes accessed | tf_op | source)
XLA Modules:
  0.0 154.7 jit_solution(3172827934905742188)
XLA Ops:
  1.4 0.1 pad_add_fusion.pick_ref
  1.5 1.3 copy.7.w_ref
  2.8 1.3 copy.8.wt_ref
  4.0 0.0 copy-start
  4.1 1.0 copy-done
  5.0 148.2 %block.1 = (bf16[128,1152]{1,0:T(8,128)(2,1)S(1)}, bf16[128,1152]{1,0:T(8,128)(2,1)S(1)}) custom-call(s32[2]{0:T(128)S(1)} %pad_add_fusion.pick_ref, bf16[128,1152]{1,0:T(8,128)(2,1)S(1)} %bitcast.10, bf16[1152,216]{1,0:T(8,128)(2,1)S(1)} %copy.7.w_ref, bf16[1152,216]{1,0:T(8,128)(2,1)S(1)} %copy.8.wt_ref, bf16[1152,1152]{1,0:T(8,128)(2,1)} %out_w_ref.1), custom_call_target="tpu_custom_call" | custom-call | tf_op jit(solution)/shard_map/block/pallas_call | solution.py:466
  153.2 0.7 copy.12
  154.0 0.7 copy.13
Async XLA Ops:
  4.0 1.0 copy-start

commit v6 on v5

--- a/solution.py
+++ b/solution.py
@@ -18,6 +18,7 @@
 CHUNKS = 2
 ROWS = BLOCK // CHUNKS
 KEY_ROWS = 16
+KEY_PAD = 80
 FRAGMENT = D // 8
 epsilon = 1e-06
 LOG2E = 1.4426950408889634
@@ -81,10 +82,11 @@
             made.wait_send()
 
 
-def greet(devices):
+def greet(devices, meanwhile):
     barrier = pltpu.get_barrier_semaphore()
     for device in devices:
         pl.semaphore_signal(barrier, inc=1, device_id=device, device_id_type=pl.DeviceIdType.MESH)
+    meanwhile()
     pl.semaphore_wait(barrier, len(devices))
 
 
@@ -194,7 +196,7 @@
     row = lax.broadcasted_iota(jnp.int32, (BLOCK, BLOCK), 0)
     column = lax.broadcasted_iota(jnp.int32, (BLOCK, BLOCK), 1)
     same = lax.rem(row, GROUP_ROWS) == lax.rem(column, GROUP_ROWS)
-    heads = range(first, first + HEAD_STEP)
+    heads = [first + i for i in range(HEAD_STEP)]
     qkv = [
         jnp.dot(
             rows, wt[h].reshape(D, 3 * HEAD_DIM), preferred_element_type=F32
@@ -262,14 +264,20 @@
     x, y, core = links.x, links.y, links.core
     others = [(dy, dc) for dy in range(4) for dc in range(2) if (dy, dc) != (0, 0)]
     turns = [(dz, dx) for dz in (0, 3, 1, 2) for dx in range(4)]
+    held = (held0, held1)
+
+    def prepare():
+        normed = rms_norm(tokens_ref[...]).astype(BF16)
+        for g in range(8):
+            slices[g] = normed[g * KEY_ROWS : (g + 1) * KEY_ROWS]
+        for c in range(CHUNKS):
+            held[c][0, 0] = normed[c * ROWS : (c + 1) * ROWS]
+
     greet(
         [links.patch_device(dx, dz) for dz, dx in turns if (dz, dx) != (0, 0)]
-        + [links.frame_at(k) for k in range(1, FRAMES)]
+        + [links.frame_at(k) for k in range(1, FRAMES)],
+        prepare,
     )
-    held = (held0, held1)
-    normed = rms_norm(tokens_ref[...]).astype(BF16)
-    for g in range(8):
-        slices[g] = normed[g * KEY_ROWS : (g + 1) * KEY_ROWS]
     picks = []
     for dy, dc in others:
         there = turn(y, dy) * 2 + lax.rem(core + dc, 2)
@@ -277,8 +285,6 @@
         picks.append(
             links.copy(slices.at[there], first.at[slot], links.frame_device(dy, 0, dc))
         )
-    for c in range(CHUNKS):
-        held[c][0, 0] = normed[c * ROWS : (c + 1) * ROWS]
     gathers = [Gather(links, held[c], ROWS) for c in range(CHUNKS)]
     gathers[0].begin_z()
     for one in gathers:
@@ -297,6 +303,7 @@
     ]
     gathers[1].begin_z()
     w[...] = jnp.zeros_like(w)
+    kt[KEY_PAD:, PATCHES:] = jnp.zeros((LANES - KEY_PAD, PATCHES), BF16)
     for i in range(3):
         w[:, i * LANES : i * LANES + HEAD_DIM] = w_ref[:, i * HEAD_DIM : (i + 1) * HEAD_DIM]
     for one in gathers:
@@ -341,20 +348,24 @@
     finish(1)
     for one in (gathers[0], gathers[1], keys):
         one.forward_x(2)
-    wt_up.wait_recv()
-    below = wt.at[x * 4 + turn(links.zh, 3), core, y]
-    wt_far = links.copy(below, below, links.patch_device(0, 1))
     for dz in range(4):
         keys.done_x(dz)
-    kv_out[...] = jnp.dot(
+    out = jnp.dot(
         kheld[...].reshape(16 * KEY_ROWS, D), w[:, LANES:], preferred_element_type=F32
-    ).astype(BF16)
+    )
+    kv_out[:KEY_PAD, :] = out[:, :LANES].T[:KEY_PAD].astype(BF16)
+    values = with_ones(out[:, LANES:]).astype(BF16)
+    kv_out[KEY_PAD:, :LANES] = values[:LANES]
+    kv_out[KEY_PAD:, LANES:] = values[LANES:]
     twin = links.frame_device(0, 0, 1)
     kv_y = [
         (links.copy(kv_out, kv_in.at[(4 - d) * 2], links.frame_device(d, 0, 0)), (4 - d) * 2)
         for d in (1, 3, 2)
     ]
     kv_twin = [links.copy(kv_out, kv_in.at[1], twin)]
+    wt_up.wait_recv()
+    below = wt.at[x * 4 + turn(links.zh, 3), core, y]
+    wt_far = links.copy(below, below, links.patch_device(0, 1))
     finish(2)
     own.wait()
     wt_down.wait_recv()
@@ -396,14 +407,15 @@
     x_down = pass_on(along_x(0), links.patch_device(3, 0))
     y_up = pass_on(along_y(0), links.frame_device(1, 0, 0))
     y_down = pass_on(along_y(0), links.frame_device(3, 0, 0))
-    cross = [pass_on(along_x(0), twin), pass_on(along_y(0), twin)]
+    cross_x, cross_y = [pass_on(along_x(0), twin)], [pass_on(along_y(0), twin)]
     kv_in[0] = kv_out[...]
     for made in kv_twin:
         made.wait_recv()
     for g in range(8):
         at = PATCHES + g * 16 * KEY_ROWS
-        kt[:, at : at + 16 * KEY_ROWS] = kv_in[g, :, :LANES].T
-        v_s[at : at + 16 * KEY_ROWS, :] = with_ones(kv_in[g, :, LANES:].astype(F32)).astype(BF16)
+        kt[:KEY_PAD, at : at + 16 * KEY_ROWS] = kv_in[g, :KEY_PAD, :]
+        v_s[at : at + LANES, :] = kv_in[g, KEY_PAD:, :LANES]
+        v_s[at + LANES : at + 2 * LANES, :] = kv_in[g, KEY_PAD:, LANES:]
     sent = []
     for g in (2, 3, 1, 0):
         scores, new = scores_of(g, slice(PATCHES, 2 * PATCHES))
@@ -431,28 +443,32 @@
     spatial = jnp.dot(rows, out_w_ref[...], preferred_element_type=F32).astype(BF16)
     spatial_ref[...] = spatial
     scatter(links, rms_norm(spatial), rows_out, rows_in)
+    y_up.wait_recv()
+    far_y = [pass_on(along_y(3, slice(0, 8)), links.frame_device(1, 0, 0))]
+    cross_y.append(pass_on(along_y(3), twin))
     x_up.wait_recv()
-    far = [pass_on(along_x(3, half=slice(0, 2)), links.patch_device(1, 0))]
-    cross.append(pass_on(along_x(3), twin))
-    y_up.wait_recv()
-    far.append(pass_on(along_y(3, slice(0, 8)), links.frame_device(1, 0, 0)))
-    cross.append(pass_on(along_y(3), twin))
+    far_x = [pass_on(along_x(3, half=slice(0, 2)), links.patch_device(1, 0))]
+    cross_x.append(pass_on(along_x(3), twin))
+    y_down.wait_recv()
+    far_y.append(pass_on(along_y(1, slice(8, 16)), links.frame_device(3, 0, 0)))
+    cross_y.append(pass_on(along_y(1), twin))
     x_down.wait_recv()
-    far.append(pass_on(along_x(1, half=slice(2, 4)), links.patch_device(3, 0)))
-    cross.append(pass_on(along_x(1), twin))
-    y_down.wait_recv()
-    far.append(pass_on(along_y(1, slice(8, 16)), links.frame_device(3, 0, 0)))
-    cross.append(pass_on(along_y(1), twin))
-    for made in far:
-        made.wait_recv()
-    cross.append(pass_on(along_x(2), twin))
-    cross.append(pass_on(along_y(2), twin))
+    far_x.append(pass_on(along_x(1, half=slice(2, 4)), links.patch_device(3, 0)))
+    cross_x.append(pass_on(along_x(1), twin))
     collect(links, rows_in, flat)
     rows = flat[...].astype(BF16)
-    for made in cross:
-        made.wait_recv()
-    for h in range(0, HEADS, HEAD_STEP):
-        mix(rows, wt, head_rows, h)
+    for made in far_y:
+        made.wait_recv()
+    cross_y.append(pass_on(along_y(2), twin))
+    for made in cross_y:
+        made.wait_recv()
+    for i, dx in enumerate((0, 3, 1, 2)):
+        if i == 1:
+            for made in far_x:
+                made.wait_recv()
+            cross_x.append(pass_on(along_x(2), twin))
+        cross_x[i].wait_recv()
+        mix(rows, wt, head_rows, turn(x, dx) * 4)
     scatter(links, head_rows[...].reshape(D, BLOCK).T, mixed_out, mixed_in)
     collect(links, mixed_in, flat)
     temporal_ref[...] = flat[...].astype(BF16)
@@ -483,8 +499,8 @@
             pltpu.VMEM((PATCHES, LANES), BF16),
             pltpu.VMEM((LANES, 2 * PATCHES), BF16),
             pltpu.VMEM((2 * PATCHES, LANES), BF16),
-            pltpu.VMEM((16 * KEY_ROWS, 2 * LANES), BF16),
-            pltpu.VMEM((8, 16 * KEY_ROWS, 2 * LANES), BF16),
+            pltpu.VMEM((KEY_PAD + LANES, 2 * LANES), BF16),
+            pltpu.VMEM((8, KEY_PAD + LANES, 2 * LANES), BF16),
             pltpu.VMEM((4, GROUP, LANES), F32),
             pltpu.VMEM((4, GROUP, LANES), F32),
             pltpu.VMEM((HEADS, HEAD_DIM, BLOCK), BF16),

time: 155 us -> 160 us (1.032)
  Pallas kernels: 148 us -> 153 us
    pallas_call x1, Pallas kernels: 148 us -> 153 us  [block(): pl.pallas_call(block_kernel, out_shape=[jax.ShapeDtypeStruct((BLOCK, D),...]
where the time goes in v6:
time: 160 us
  Pallas kernels  153 us (96%)
  local copies, waits for them, and re-layouts  4.92 us (3%)
    pallas_call x1, Pallas kernels, block(): pl.pallas_call(block_kernel, out_shape=[jax.ShapeDtypeStruct((BLOCK, D),...  153 us
    unnamed x6, local copies, waits for them, and re-layouts  4.92 us

profile of v6, /device:TPU:1, one launch (start us, length us, event | category | flops | bytes accessed | tf_op | source)
XLA Modules:
  0.0 159.6 jit_solution(810802995573133733)
XLA Ops:
  1.4 0.1 pad_add_fusion.pick_ref
  1.5 1.3 copy.7.w_ref
  2.8 1.3 copy.8.wt_ref
  4.0 0.0 copy-start
  4.1 1.0 copy-done
  5.0 153.1 %block.1 = (bf16[128,1152]{1,0:T(8,128)(2,1)S(1)}, bf16[128,1152]{1,0:T(8,128)(2,1)S(1)}) custom-call(s32[2]{0:T(128)S(1)} %pad_add_fusion.pick_ref, bf16[128,1152]{1,0:T(8,128)(2,1)S(1)} %bitcast.10, bf16[1152,216]{1,0:T(8,128)(2,1)S(1)} %copy.7.w_ref, bf16[1152,216]{1,0:T(8,128)(2,1)S(1)} %copy.8.wt_ref, bf16[1152,1152]{1,0:T(8,128)(2,1)} %out_w_ref.1), custom_call_target="tpu_custom_call" | custom-call | tf_op jit(solution)/shard_map/block/pallas_call | solution.py:482
  158.1 0.7 copy.12
  158.8 0.7 copy.13
Async XLA Ops:
  4.0 1.0 copy-start

commit v7 on v5

--- a/solution.py
+++ b/solution.py
@@ -18,6 +18,7 @@
 CHUNKS = 2
 ROWS = BLOCK // CHUNKS
 KEY_ROWS = 16
+KEY_PAD = 80
 FRAGMENT = D // 8
 epsilon = 1e-06
 LOG2E = 1.4426950408889634
@@ -81,10 +82,11 @@
             made.wait_send()
 
 
-def greet(devices):
+def greet(devices, meanwhile):
     barrier = pltpu.get_barrier_semaphore()
     for device in devices:
         pl.semaphore_signal(barrier, inc=1, device_id=device, device_id_type=pl.DeviceIdType.MESH)
+    meanwhile()
     pl.semaphore_wait(barrier, len(devices))
 
 
@@ -262,14 +264,20 @@
     x, y, core = links.x, links.y, links.core
     others = [(dy, dc) for dy in range(4) for dc in range(2) if (dy, dc) != (0, 0)]
     turns = [(dz, dx) for dz in (0, 3, 1, 2) for dx in range(4)]
+    held = (held0, held1)
+
+    def prepare():
+        normed = rms_norm(tokens_ref[...]).astype(BF16)
+        for g in range(8):
+            slices[g] = normed[g * KEY_ROWS : (g + 1) * KEY_ROWS]
+        for c in range(CHUNKS):
+            held[c][0, 0] = normed[c * ROWS : (c + 1) * ROWS]
+
     greet(
         [links.patch_device(dx, dz) for dz, dx in turns if (dz, dx) != (0, 0)]
-        + [links.frame_at(k) for k in range(1, FRAMES)]
+        + [links.frame_at(k) for k in range(1, FRAMES)],
+        prepare,
     )
-    held = (held0, held1)
-    normed = rms_norm(tokens_ref[...]).astype(BF16)
-    for g in range(8):
-        slices[g] = normed[g * KEY_ROWS : (g + 1) * KEY_ROWS]
     picks = []
     for dy, dc in others:
         there = turn(y, dy) * 2 + lax.rem(core + dc, 2)
@@ -277,8 +285,6 @@
         picks.append(
             links.copy(slices.at[there], first.at[slot], links.frame_device(dy, 0, dc))
         )
-    for c in range(CHUNKS):
-        held[c][0, 0] = normed[c * ROWS : (c + 1) * ROWS]
     gathers = [Gather(links, held[c], ROWS) for c in range(CHUNKS)]
     gathers[0].begin_z()
     for one in gathers:
@@ -297,6 +303,7 @@
     ]
     gathers[1].begin_z()
     w[...] = jnp.zeros_like(w)
+    kt[KEY_PAD:, PATCHES:] = jnp.zeros((LANES - KEY_PAD, PATCHES), BF16)
     for i in range(3):
         w[:, i * LANES : i * LANES + HEAD_DIM] = w_ref[:, i * HEAD_DIM : (i + 1) * HEAD_DIM]
     for one in gathers:
@@ -346,9 +353,13 @@
     wt_far = links.copy(below, below, links.patch_device(0, 1))
     for dz in range(4):
         keys.done_x(dz)
-    kv_out[...] = jnp.dot(
+    out = jnp.dot(
         kheld[...].reshape(16 * KEY_ROWS, D), w[:, LANES:], preferred_element_type=F32
-    ).astype(BF16)
+    )
+    kv_out[:KEY_PAD, :] = out[:, :LANES].T[:KEY_PAD].astype(BF16)
+    values = with_ones(out[:, LANES:]).astype(BF16)
+    kv_out[KEY_PAD:, :LANES] = values[:LANES]
+    kv_out[KEY_PAD:, LANES:] = values[LANES:]
     twin = links.frame_device(0, 0, 1)
     kv_y = [
         (links.copy(kv_out, kv_in.at[(4 - d) * 2], links.frame_device(d, 0, 0)), (4 - d) * 2)
@@ -402,8 +413,9 @@
         made.wait_recv()
     for g in range(8):
         at = PATCHES + g * 16 * KEY_ROWS
-        kt[:, at : at + 16 * KEY_ROWS] = kv_in[g, :, :LANES].T
-        v_s[at : at + 16 * KEY_ROWS, :] = with_ones(kv_in[g, :, LANES:].astype(F32)).astype(BF16)
+        kt[:KEY_PAD, at : at + 16 * KEY_ROWS] = kv_in[g, :KEY_PAD, :]
+        v_s[at : at + LANES, :] = kv_in[g, KEY_PAD:, :LANES]
+        v_s[at + LANES : at + 2 * LANES, :] = kv_in[g, KEY_PAD:, LANES:]
     sent = []
     for g in (2, 3, 1, 0):
         scores, new = scores_of(g, slice(PATCHES, 2 * PATCHES))
@@ -483,8 +495,8 @@
             pltpu.VMEM((PATCHES, LANES), BF16),
             pltpu.VMEM((LANES, 2 * PATCHES), BF16),
             pltpu.VMEM((2 * PATCHES, LANES), BF16),
-            pltpu.VMEM((16 * KEY_ROWS, 2 * LANES), BF16),
-            pltpu.VMEM((8, 16 * KEY_ROWS, 2 * LANES), BF16),
+            pltpu.VMEM((KEY_PAD + LANES, 2 * LANES), BF16),
+            pltpu.VMEM((8, KEY_PAD + LANES, 2 * LANES), BF16),
             pltpu.VMEM((4, GROUP, LANES), F32),
             pltpu.VMEM((4, GROUP, LANES), F32),
             pltpu.VMEM((HEADS, HEAD_DIM, BLOCK), BF16),

time: 155 us -> 155 us (level)
  no operation moved by 1% of the time
where the time goes in v7:
time: 155 us; the launch traced here: 154 us
  Pallas kernels  148 us (95%)
  local copies, waits for them, and re-layouts  4.92 us (3%)
    pallas_call x1, Pallas kernels, block(): pl.pallas_call(block_kernel, out_shape=[jax.ShapeDtypeStruct((BLOCK, D),...  148 us
    unnamed x6, local copies, waits for them, and re-layouts  4.92 us

profile of v7, /device:TPU:1, one launch (start us, length us, event | category | flops | bytes accessed | tf_op | source)
XLA Modules:
  0.0 154.5 jit_solution(15881990423955234268)
XLA Ops:
  1.4 0.1 pad_add_fusion.pick_ref
  1.5 1.3 copy.7.w_ref
  2.8 1.3 copy.8.wt_ref
  4.0 0.0 copy-start
  4.1 1.0 copy-done
  5.0 148.0 %block.1 = (bf16[128,1152]{1,0:T(8,128)(2,1)S(1)}, bf16[128,1152]{1,0:T(8,128)(2,1)S(1)}) custom-call(s32[2]{0:T(128)S(1)} %pad_add_fusion.pick_ref, bf16[128,1152]{1,0:T(8,128)(2,1)S(1)} %bitcast.10, bf16[1152,216]{1,0:T(8,128)(2,1)S(1)} %copy.7.w_ref, bf16[1152,216]{1,0:T(8,128)(2,1)S(1)} %copy.8.wt_ref, bf16[1152,1152]{1,0:T(8,128)(2,1)} %out_w_ref.1), custom_call_target="tpu_custom_call" | custom-call | tf_op jit(solution)/shard_map/block/pallas_call | solution.py:478
  153.1 0.7 copy.12
  153.8 0.7 copy.13
Async XLA Ops:
  4.0 1.0 copy-start
